TPU v7x, 32 devices: a whole 2x2x4 slice. The times are simulated.
32 devices in a mesh: dp: 8 (over z, x), blk: 4 (over y, core).
Axes of the slice: x: 2, y: 2, z: 4, core: 2. Of those that a mesh axis runs over, the one named last changes fastest.
Arguments:
- tokens: bfloat16 [64, 512, 768], P('dp', 'blk'), may hold values from -6 to 6
- fragments: int32 [64, 512], P('dp', 'blk'), may hold values from 0 to 511, as said below
- cotangent: bfloat16 [64, 512, 768], P('dp', 'blk'), may hold values from -6 to 6
- query_weight: bfloat16 [768, 768], P('dp'), may hold values from -0.21875 to 0.21875
- query_bias: bfloat16 [768], P('dp'), may hold values from -1.75 to 1.75
- key_weight: bfloat16 [768, 768], P('dp'), may hold values from -0.21875 to 0.21875
- value_weight: bfloat16 [768, 768], P('dp'), may hold values from -0.21875 to 0.21875
- value_bias: bfloat16 [768], P('dp'), may hold values from -1.75 to 1.75
- out_weight: bfloat16 [768, 768], P('dp'), may hold values from -1.25 to 1.25
- out_bias: bfloat16 [768], P('dp'), may hold values from -1.75 to 1.75
- first_gain: bfloat16 [768], P('dp'), may hold values from 0.5 to 1.5
- first_shift: bfloat16 [768], P('dp'), may hold values from -1.75 to 1.75
- up_weight: bfloat16 [768, 3072], P('dp'), may hold values from -0.21875 to 0.21875
- up_bias: bfloat16 [3072], P('dp'), may hold values from -1.75 to 1.75
- down_weight: bfloat16 [3072, 768], P('dp'), may hold values from -0.109375 to 0.109375
- down_bias: bfloat16 [768], P('dp'), may hold values from -1.75 to 1.75
- second_gain: bfloat16 [768], P('dp'), may hold values from 0.5 to 1.5
- second_shift: bfloat16 [768], P('dp'), may hold values from -1.75 to 1.75
Outputs:
- output: bfloat16 [64, 512, 768], P('dp', 'blk')
- grad_tokens: bfloat16 [64, 512, 768], P('dp', 'blk')
- query_weight_gradient: float32 [768, 768], P('dp')
- grad_query_bias: float32 [768], P('dp')
- grad_key_weight: float32 [768, 768], P('dp')
- grad_value_weight: float32 [768, 768], P('dp')
- grad_value_bias: float32 [768], P('dp')
- grad_out_weight: float32 [768, 768], P('dp')
- grad_out_bias: float32 [768], P('dp')
- grad_first_gain: float32 [768], P('dp')
- grad_first_shift: float32 [768], P('dp')
- grad_up_weight: float32 [768, 3072], P('dp')
- grad_up_bias: float32 [3072], P('dp')
- grad_down_weight: float32 [3072, 768], P('dp')
- grad_down_bias: float32 [768], P('dp')
- grad_second_gain: float32 [768], P('dp')
- grad_second_shift: float32 [768], P('dp')
Inputs may be any that keep to these rules, and one draw needn't show every extreme that they name: `fragments`: fragment ids never fall along a row; the last position of every row is a fragment of its own with id 512 - 1.
All inputs are finite; a program needn't handle non-finite values.
Results may differ from a plain program's by a relative error of at most 0.024.
Values may be sent and summed in bfloat16 or wider, within the bound.
No kernel may reach another device: no remote copies, remote signals or barrier semaphores. Data moves between devices by JAX's collectives and lax.ppermute only.
A program may use at most 256 MiB of HBM per device.

v0:
```python
import jax
import jax.numpy as jnp
from jax import lax
from jax.sharding import PartitionSpec as P

H = 12
DH = 64
MB = 2


EPS = 1e-12
NEG = -1e30
ROOT_HALF = 0.7071067811865476
DENSITY = 0.3989422804014327


def matmul(input_tokens, weight_matrix):
    return jnp.einsum(
        "cfh,hv->cfv", input_tokens, weight_matrix, preferred_element_type=jnp.float32
    )


def matmul_back(gradient_bundle, weight_matrix):
    return jnp.einsum(
        "gok,vk->gov", gradient_bundle, weight_matrix, preferred_element_type=jnp.float32
    )


def outer_sum(input_tokens, gradient_bundle):
    return jnp.einsum(
        "ubc,ubj->cj", input_tokens, gradient_bundle, preferred_element_type=jnp.float32
    )


def row_total(gradient_bundle):
    return jnp.sum(gradient_bundle.astype(jnp.float32), axis=(0, 1))


def normalize(input_tokens):
    center = input_tokens - jnp.mean(input_tokens, axis=-1, keepdims=True)
    inverse = lax.rsqrt(jnp.mean(center * center, axis=-1, keepdims=True) + EPS)
    return (center * inverse, inverse)


def normalize_back(grad_normed, normalized_rows, inverse):
    return inverse * (
        grad_normed
        - jnp.mean(grad_normed, axis=-1, keepdims=True)
        - normalized_rows * jnp.mean(grad_normed * normalized_rows, axis=-1, keepdims=True)
    )


def micro_batch(weights, input_tokens, query_ids, all_ids, cotangent):
    (
        query_weight,
        query_bias,
        key_weight,
        value_weight,
        value_bias,
        out_weight,
        out_bias,
        first_gain,
        first_shift,
        up_weight,
        up_bias,
        down_weight,
        down_bias,
        second_gain,
        second_shift,
    ) = weights
    row_count, span_len, feat_dim = input_tokens.shape
    factor = DH ** (-0.5)
    queries = (matmul(input_tokens, query_weight) + query_bias.astype(jnp.float32)).astype(
        jnp.bfloat16
    )
    keys = matmul(input_tokens, key_weight).astype(jnp.bfloat16)
    values = (matmul(input_tokens, value_weight) + value_bias.astype(jnp.float32)).astype(
        jnp.bfloat16
    )
    query_heads = queries.reshape(row_count, span_len, H, DH)

    def block_scores(pieces):
        key_piece, value_piece = pieces
        width_now = key_piece.shape[1]
        key_heads = key_piece.reshape(row_count, width_now, H, DH)
        value_heads = value_piece.reshape(row_count, width_now, H, DH)
        allowed = (query_ids[:, :, None] == all_ids[:, None, :])[:, None]
        scores = (
            jnp.einsum(
                "schd,snhd->shcn", query_heads, key_heads, preferred_element_type=jnp.float32
            )
            * factor
        )
        return (key_heads, value_heads, allowed, scores)

    running = jnp.full((row_count, H, span_len), NEG, jnp.float32)
    key_heads, value_heads, allowed, scores = block_scores(
        (
            lax.all_gather(keys, "blk", axis=1, tiled=True),
            lax.all_gather(values, "blk", axis=1, tiled=True),
        )
    )
    scores = jnp.where(allowed, scores, NEG)
    newest = jnp.maximum(running, jnp.max(scores, axis=-1))
    weights_now = jnp.where(allowed, jnp.exp(scores - newest[..., None]), 0.0)
    totals = jnp.sum(weights_now, axis=-1)
    update = jnp.einsum(
        "shcn,snhd->schd",
        weights_now.astype(jnp.bfloat16),
        value_heads,
        preferred_element_type=jnp.float32,
    )
    accum = update
    running, totals, accum = (newest, totals, accum)
    attended_full = (accum / jnp.transpose(totals, (0, 2, 1))[..., None]).reshape(
        row_count, span_len, feat_dim
    )
    log_total = running + jnp.log(totals)
    attended = attended_full.astype(jnp.bfloat16)
    branch = matmul(attended, out_weight) + out_bias.astype(jnp.float32)
    first_normed, first_inverse = normalize(input_tokens.astype(jnp.float32) + branch)
    hidden = first_normed * first_gain.astype(jnp.float32) + first_shift.astype(jnp.float32)
    hidden_low = hidden.astype(jnp.bfloat16)
    before = matmul(hidden_low, up_weight) + up_bias.astype(jnp.float32)
    active = jax.nn.gelu(before, approximate=False).astype(jnp.bfloat16)
    second = matmul(active, down_weight) + down_bias.astype(jnp.float32)
    second_normed, second_inverse = normalize(hidden + second)
    result = (
        second_normed * second_gain.astype(jnp.float32) + second_shift.astype(jnp.float32)
    ).astype(jnp.bfloat16)
    grad_out = cotangent.astype(jnp.float32)
    grad_second_shift = jnp.sum(grad_out, axis=(0, 1))
    grad_second_gain = jnp.sum(grad_out * second_normed, axis=(0, 1))
    grad_r2 = normalize_back(
        grad_out * second_gain.astype(jnp.float32), second_normed, second_inverse
    )
    grad_second = grad_r2.astype(jnp.bfloat16)
    grad_down_bias = row_total(grad_second)
    grad_down_weight = outer_sum(active, grad_second)
    slope = 0.5 * (1.0 + lax.erf(before * ROOT_HALF)) + before * DENSITY * jnp.exp(
        -0.5 * before * before
    )
    grad_before = (matmul_back(grad_second, down_weight) * slope).astype(jnp.bfloat16)
    grad_up_bias = row_total(grad_before)
    grad_up_weight = outer_sum(hidden_low, grad_before)
    grad_hidden = grad_r2 + matmul_back(grad_before, up_weight)
    grad_first_shift = jnp.sum(grad_hidden, axis=(0, 1))
    grad_first_gain = jnp.sum(grad_hidden * first_normed, axis=(0, 1))
    grad_r1 = normalize_back(
        grad_hidden * first_gain.astype(jnp.float32), first_normed, first_inverse
    )
    grad_branch = grad_r1.astype(jnp.bfloat16)
    grad_out_bias = row_total(grad_branch)
    grad_out_weight = outer_sum(attended, grad_branch)
    grad_attended = matmul_back(grad_branch, out_weight).astype(jnp.bfloat16)
    grad_heads = grad_attended.reshape(row_count, span_len, H, DH)
    delta = jnp.sum(
        (grad_attended.astype(jnp.float32) * attended_full).reshape(row_count, span_len, H, DH),
        axis=-1,
    )
    delta = jnp.transpose(delta, (0, 2, 1))
    key_heads, value_heads, allowed, scores = block_scores(
        (
            lax.all_gather(keys, "blk", axis=1, tiled=True),
            lax.all_gather(values, "blk", axis=1, tiled=True),
        )
    )
    width_now = key_heads.shape[1]
    probs = jnp.where(allowed, jnp.exp(scores - log_total[..., None]), 0.0)
    grad_value_part = jnp.einsum(
        "shcn,schd->snhd",
        probs.astype(jnp.bfloat16),
        grad_heads,
        preferred_element_type=jnp.float32,
    )
    grad_probs = jnp.einsum(
        "schd,snhd->shcn", grad_heads, value_heads, preferred_element_type=jnp.float32
    )
    grad_scores = (probs * (grad_probs - delta[..., None])).astype(jnp.bfloat16)
    grad_query_acc = (
        jnp.einsum("shcn,snhd->schd", grad_scores, key_heads, preferred_element_type=jnp.float32)
        * factor
    )
    grad_key_part = (
        jnp.einsum("shcn,schd->snhd", grad_scores, query_heads, preferred_element_type=jnp.float32)
        * factor
    )
    key_gradient_gathered_total = grad_key_part.reshape(row_count, width_now, feat_dim)
    grad_value_all = grad_value_part.reshape(row_count, width_now, feat_dim)
    grad_query_acc, key_gradient_gathered_total, grad_value_all = (
        grad_query_acc,
        key_gradient_gathered_total,
        grad_value_all,
    )
    grad_key_sum, grad_value_sum = (
        lax.psum_scatter(
            key_gradient_gathered_total.astype(jnp.bfloat16), "blk", scatter_dimension=1, tiled=True
        ).astype(jnp.float32),
        lax.psum_scatter(
            grad_value_all.astype(jnp.bfloat16), "blk", scatter_dimension=1, tiled=True
        ).astype(jnp.float32),
    )
    grad_queries = grad_query_acc.reshape(row_count, span_len, feat_dim).astype(jnp.bfloat16)
    grad_keys = grad_key_sum.astype(jnp.bfloat16)
    grad_values = grad_value_sum.astype(jnp.bfloat16)
    grad_query_bias = row_total(grad_queries)
    grad_value_bias = row_total(grad_values)
    query_weight_gradient = outer_sum(input_tokens, grad_queries)
    grad_key_weight = outer_sum(input_tokens, grad_keys)
    grad_value_weight = outer_sum(input_tokens, grad_values)
    grad_inputs = (
        grad_r1
        + matmul_back(grad_queries, query_weight)
        + matmul_back(grad_keys, key_weight)
        + matmul_back(grad_values, value_weight)
    ).astype(jnp.bfloat16)
    gradient_bundle = (
        query_weight_gradient,
        grad_query_bias,
        grad_key_weight,
        grad_value_weight,
        grad_value_bias,
        grad_out_weight,
        grad_out_bias,
        grad_first_gain,
        grad_first_shift,
        grad_up_weight,
        grad_up_bias,
        grad_down_weight,
        grad_down_bias,
        grad_second_gain,
        grad_second_shift,
    )
    return (result, grad_inputs, gradient_bundle)


def local(
    tokens,
    fragments,
    cotangent,
    query_weight,
    query_bias,
    key_weight,
    value_weight,
    value_bias,
    out_weight,
    out_bias,
    first_gain,
    first_shift,
    up_weight,
    up_bias,
    down_weight,
    down_bias,
    second_gain,
    second_shift,
):
    rows_each = tokens.shape[0] // MB
    data_count = lax.axis_size("dp")
    all_ids = lax.all_gather(fragments, "blk", axis=1, tiled=True)
    shard_shapes = (
        query_weight,
        query_bias,
        key_weight,
        value_weight,
        value_bias,
        out_weight,
        out_bias,
        first_gain,
        first_shift,
        up_weight,
        up_bias,
        down_weight,
        down_bias,
        second_gain,
        second_shift,
    )
    totals = tuple(
        (
            jnp.zeros((item.shape[0] * data_count,) + item.shape[1:], jnp.float32)
            for item in shard_shapes
        )
    )
    results = []
    grad_parts = []
    for loop_step_index in range(MB):
        gathered = (
            lax.all_gather(query_weight, "dp", axis=0, tiled=True),
            lax.all_gather(query_bias, "dp", axis=0, tiled=True),
            lax.all_gather(key_weight, "dp", axis=0, tiled=True),
            lax.all_gather(value_weight, "dp", axis=0, tiled=True),
            lax.all_gather(value_bias, "dp", axis=0, tiled=True),
            lax.all_gather(out_weight, "dp", axis=0, tiled=True),
            lax.all_gather(out_bias, "dp", axis=0, tiled=True),
            lax.all_gather(first_gain, "dp", axis=0, tiled=True),
            lax.all_gather(first_shift, "dp", axis=0, tiled=True),
            lax.all_gather(up_weight, "dp", axis=0, tiled=True),
            lax.all_gather(up_bias, "dp", axis=0, tiled=True),
            lax.all_gather(down_weight, "dp", axis=0, tiled=True),
            lax.all_gather(down_bias, "dp", axis=0, tiled=True),
            lax.all_gather(second_gain, "dp", axis=0, tiled=True),
            lax.all_gather(second_shift, "dp", axis=0, tiled=True),
        )
        lower = loop_step_index * rows_each
        upper = lower + rows_each
        result, grad_inputs, gradient_bundle = micro_batch(
            gathered,
            tokens[lower:upper],
            fragments[lower:upper],
            all_ids[lower:upper],
            cotangent[lower:upper],
        )
        results.append(result)
        grad_parts.append(grad_inputs)
        totals = tuple((left + right for left, right in zip(totals, gradient_bundle)))
    partial_sums = (
        lax.psum_scatter(
            totals[0].astype(jnp.bfloat16), "dp", scatter_dimension=0, tiled=True
        ).astype(jnp.float32),
        lax.psum_scatter(
            totals[1].astype(jnp.bfloat16), "dp", scatter_dimension=0, tiled=True
        ).astype(jnp.float32),
        lax.psum_scatter(
            totals[2].astype(jnp.bfloat16), "dp", scatter_dimension=0, tiled=True
        ).astype(jnp.float32),
        lax.psum_scatter(
            totals[3].astype(jnp.bfloat16), "dp", scatter_dimension=0, tiled=True
        ).astype(jnp.float32),
        lax.psum_scatter(
            totals[4].astype(jnp.bfloat16), "dp", scatter_dimension=0, tiled=True
        ).astype(jnp.float32),
        lax.psum_scatter(
            totals[5].astype(jnp.bfloat16), "dp", scatter_dimension=0, tiled=True
        ).astype(jnp.float32),
        lax.psum_scatter(
            totals[6].astype(jnp.bfloat16), "dp", scatter_dimension=0, tiled=True
        ).astype(jnp.float32),
        lax.psum_scatter(
            totals[7].astype(jnp.bfloat16), "dp", scatter_dimension=0, tiled=True
        ).astype(jnp.float32),
        lax.psum_scatter(
            totals[8].astype(jnp.bfloat16), "dp", scatter_dimension=0, tiled=True
        ).astype(jnp.float32),
        lax.psum_scatter(
            totals[9].astype(jnp.bfloat16), "dp", scatter_dimension=0, tiled=True
        ).astype(jnp.float32),
        lax.psum_scatter(
            totals[10].astype(jnp.bfloat16), "dp", scatter_dimension=0, tiled=True
        ).astype(jnp.float32),
        lax.psum_scatter(
            totals[11].astype(jnp.bfloat16), "dp", scatter_dimension=0, tiled=True
        ).astype(jnp.float32),
        lax.psum_scatter(
            totals[12].astype(jnp.bfloat16), "dp", scatter_dimension=0, tiled=True
        ).astype(jnp.float32),
        lax.psum_scatter(
            totals[13].astype(jnp.bfloat16), "dp", scatter_dimension=0, tiled=True
        ).astype(jnp.float32),
        lax.psum_scatter(
            totals[14].astype(jnp.bfloat16), "dp", scatter_dimension=0, tiled=True
        ).astype(jnp.float32),
    )
    shards = (
        lax.psum(partial_sums[0].astype(jnp.bfloat16), "blk").astype(jnp.float32),
        lax.psum(partial_sums[1].astype(jnp.bfloat16), "blk").astype(jnp.float32),
        lax.psum(partial_sums[2].astype(jnp.bfloat16), "blk").astype(jnp.float32),
        lax.psum(partial_sums[3].astype(jnp.bfloat16), "blk").astype(jnp.float32),
        lax.psum(partial_sums[4].astype(jnp.bfloat16), "blk").astype(jnp.float32),
        lax.psum(partial_sums[5].astype(jnp.bfloat16), "blk").astype(jnp.float32),
        lax.psum(partial_sums[6].astype(jnp.bfloat16), "blk").astype(jnp.float32),
        lax.psum(partial_sums[7].astype(jnp.bfloat16), "blk").astype(jnp.float32),
        lax.psum(partial_sums[8].astype(jnp.bfloat16), "blk").astype(jnp.float32),
        lax.psum(partial_sums[9].astype(jnp.bfloat16), "blk").astype(jnp.float32),
        lax.psum(partial_sums[10].astype(jnp.bfloat16), "blk").astype(jnp.float32),
        lax.psum(partial_sums[11].astype(jnp.bfloat16), "blk").astype(jnp.float32),
        lax.psum(partial_sums[12].astype(jnp.bfloat16), "blk").astype(jnp.float32),
        lax.psum(partial_sums[13].astype(jnp.bfloat16), "blk").astype(jnp.float32),
        lax.psum(partial_sums[14].astype(jnp.bfloat16), "blk").astype(jnp.float32),
    )
    return (
        jnp.concatenate(results, axis=0),
        jnp.concatenate(grad_parts, axis=0),
        shards[0],
        shards[1],
        shards[2],
        shards[3],
        shards[4],
        shards[5],
        shards[6],
        shards[7],
        shards[8],
        shards[9],
        shards[10],
        shards[11],
        shards[12],
        shards[13],
        shards[14],
    )


def solution(mesh):
    placed = (
        P("dp", "blk", None),
        P("dp", "blk"),
        P("dp", "blk", None),
        P("dp", None),
        P("dp"),
        P("dp", None),
        P("dp", None),
        P("dp"),
        P("dp", None),
        P("dp"),
        P("dp"),
        P("dp"),
        P("dp", None),
        P("dp"),
        P("dp", None),
        P("dp"),
        P("dp"),
        P("dp"),
    )
    return jax.shard_map(
        local,
        mesh=mesh,
        in_specs=placed,
        out_specs=(
            P("dp", "blk", None),
            P("dp", "blk", None),
            P("dp", None),
            P("dp"),
            P("dp", None),
            P("dp", None),
            P("dp"),
            P("dp", None),
            P("dp"),
            P("dp"),
            P("dp"),
            P("dp", None),
            P("dp"),
            P("dp", None),
            P("dp"),
            P("dp"),
            P("dp"),
        ),
        check_vma=False,
    )
```

profile of v0, /device:TPU:0, one launch (start us, length us, event | category | flops | bytes accessed | tf_op | source)
XLA Modules:
  0.0 1229.6 jit_solution(2003493102858217830)
XLA Ops:
  9.6 44.5 %all-gather.18.cloned.1.call-done = bf16[768,768]{1,0:T(8,128)(2,1)} async-done(((bf16[96,768]{1,0:T(8,128)(2,1)}), bf16[768,768]{1,0:T(8,128)(2,1)}) %all-gather.18.cloned.1.call-update) | async-done | bytes 1179664 | tf_op jit(solution)/shard_map/all_gather | solution.py:289
  60.3 35.6 %all-reduce.18 = (bf16[768]{0:T(1024)(128)(2,1)S(1)}, bf16[768]{0:T(1024)(128)(2,1)S(1)}, bf16[768]{0:T(1024)(128)(2,1)S(1)}, bf16[768]{0:T(1024)(128)(2,1)S(1)}...) all-reduce(bf16[768]{0:T(1024)(128)(2,1)S(1)} %dynamic-update-slice, ...), channel_id=1, replica_groups=mesh['dp'=8,'blk'=4] {'dp'}, use_global_device_ids=true, to_apply=%add.1 | all-reduce | flops 5376 | bytes 21504
  106.1 5.2 all_gather.82
  111.3 26.0 %all-gather = bf16[8,1,384]{2,1,0:T(2,128)(2,1)S(1)} all-gather(bf16[1,1,384]{2,1,0:T(2,128)(2,1)S(1)} %reshape.243), channel_id=1, replica_groups=mesh['dp'=8,'blk'=4] {'dp'}, dimensions={0}, use_global_device_ids=true | all-gather | bytes 6912 | tf_op jit(solution)/shard_map/all_gather | solution.py:297
  144.9 22.9 %all-gather.30.cloned.1.call-done = bf16[4,512,768]{2,1,0:T(8,128)(2,1)} async-done(((bf16[4,128,768]{2,1,0:T(8,128)(2,1)}), bf16[4,512,768]{2,1,0:T(8,128)(2,1)}) %all-gather.30.cloned.1.call-update) | async-done | bytes 3145744 | tf_op jit(solution)/shard_map/all_gather | solution.py:99
  180.5 17.8 %all-gather.28.cloned.1.call-done = bf16[4,512,768]{2,1,0:T(8,128)(2,1)} async-done(((bf16[4,128,768]{2,1,0:T(8,128)(2,1)}), bf16[4,512,768]{2,1,0:T(8,128)(2,1)}) %all-gather.28.cloned.1.call-update) | async-done | bytes 3145744 | tf_op jit(solution)/shard_map/all_gather | solution.py:100
  198.3 4.7 copy.99
  203.0 7.4 bitcast_divide_fusion
  212.2 29.3 %all-gather.22.cloned.1.call-done = bf16[768,768]{1,0:T(8,128)(2,1)} async-done(((bf16[96,768]{1,0:T(8,128)(2,1)}), bf16[768,768]{1,0:T(8,128)(2,1)}) %all-gather.22.cloned.1.call-update) | async-done | bytes 1179664 | tf_op jit(solution)/shard_map/all_gather | solution.py:292
  245.1 25.2 %all-gather.20.cloned.1.call-done = bf16[4,512,768]{2,1,0:T(8,128)(2,1)} async-done(((bf16[4,128,768]{2,1,0:T(8,128)(2,1)}), bf16[4,512,768]{2,1,0:T(8,128)(2,1)}) %all-gather.20.cloned.1.call-update) | async-done | bytes 3145744 | tf_op jit(solution)/shard_map/all_gather | solution.py:99
  278.2 5.0 copy-done.1
  287.3 13.7 %all-gather.14.cloned.1.call-done = bf16[4,512,768]{2,1,0:T(8,128)(2,1)} async-done(((bf16[4,128,768]{2,1,0:T(8,128)(2,1)}), bf16[4,512,768]{2,1,0:T(8,128)(2,1)}) %all-gather.14.cloned.1.call-update) | async-done | bytes 3145744 | tf_op jit(solution)/shard_map/all_gather | solution.py:100
  301.1 5.1 copy.95
  306.2 7.9 bitcast_divide_fusion.1
  315.4 67.8 %all-gather.24.cloned.1.call-done = bf16[768,3072]{1,0:T(8,128)(2,1)} async-done(((bf16[96,3072]{1,0:T(8,128)(2,1)}), bf16[768,3072]{1,0:T(8,128)(2,1)}) %all-gather.24.cloned.1.call-update) | async-done | bytes 4718608 | tf_op jit(solution)/shard_map/all_gather | solution.py:296
  383.2 5.3 fusion.64
  388.5 6.8 fusion.94
  398.0 30.3 %fusion.10 = (bf16[4,128,3072]{2,1,0:T(8,128)(2,1)}, bf16[4,128,3072]{2,1,0:T(8,128)(2,1)}) fusion(f32[4,128,3072]{2,1,0:T(8,128)S(1)} %get-tuple-element.162, f32[3072]{0:T(1024)S(1)} %bitcast.307, u8[128,3072]{1,0:T(8,128)(4,1)S(1)} %get-tuple-element.69, u8[128,3072]{1,0:T(8,128)(4,1)S(1)} %get-tuple-element.68, ...), kind=kLoop, calls=%fused_computation.24 | loop fusion | flops 221773824 | bytes 20459520 | tf_op jit(solution)/shard_map/convert_element_type | solution.py:125
  428.3 34.9 %all-gather.26.cloned.1.call-done = bf16[3072,768]{1,0:T(8,128)(2,1)} async-done(((bf16[384,768]{1,0:T(8,128)(2,1)}), bf16[3072,768]{1,0:T(8,128)(2,1)}) %all-gather.26.cloned.1.call-update) | async-done | bytes 4718608 | tf_op jit(solution)/shard_map/all_gather | solution.py:298
  463.3 6.6 fusion.177
  477.4 9.6 convert_reduce_fusion
  487.0 5.9 multiply_reduce_fusion
  493.0 7.3 convert_reduce_fusion.1
  500.3 5.3 convert_reduce_fusion.6
  514.9 8.2 multiply_convert_fusion
  526.7 6.0 copy.138
  548.1 8.7 multiply_convert_fusion.1
  560.5 4.7 copy.134
  568.8 7.3 fusion.72
  576.2 4.7 copy.136
  584.5 7.5 fusion.75
  592.0 4.8 copy.140
  601.1 5.8 convert_reduce_fusion.11
  609.1 5.8 convert_reduce_fusion.10
  628.9 25.4 %reduce-scatter.33.cloned.1.call-done = bf16[128,3072]{1,0:T(8,128)(2,1)} async-done(((bf16[512,3072]{1,0:T(8,128)(2,1)}), bf16[128,3072]{1,0:T(8,128)(2,1)}) %reduce-scatter.33.cloned.1.call-update) | async-done | bytes 786448
  657.0 37.9 %reduce-scatter.37.cloned.1.call-done = bf16[128,3072]{1,0:T(8,128)(2,1)} async-done(((bf16[512,3072]{1,0:T(8,128)(2,1)}), bf16[128,3072]{1,0:T(8,128)(2,1)}) %reduce-scatter.37.cloned.1.call-update) | async-done | bytes 786448
  708.7 4.9 fusion.155
  713.7 4.9 fusion.3
  719.8 4.7 fusion.179
  737.1 25.7 %reduce-scatter.39.cloned.1.call-done = bf16[96,768]{1,0:T(8,128)(2,1)} async-done(((bf16[768,768]{1,0:T(8,128)(2,1)}), bf16[96,768]{1,0:T(8,128)(2,1)}) %reduce-scatter.39.cloned.1.call-update) | async-done | bytes 147472
  767.1 35.7 %all-reduce.17 = (bf16[768]{0:T(1024)(128)(2,1)S(1)}, bf16[768]{0:T(1024)(128)(2,1)}, bf16[768]{0:T(1024)(128)(2,1)}, bf16[768]{0:T(1024)(128)(2,1)}, bf16[768]{...) all-reduce(bf16[768]{0:T(1024)(128)(2,1)S(1)} %dynamic-update-slice, ...), channel_id=1, replica_groups=mesh['dp'=8,'blk'=4] {'dp'}, use_global_device_ids=true, to_apply=%add.7 | all-reduce | flops 9984 | bytes 39936
  810.3 19.4 %reduce-scatter.41.cloned.1.call-done = bf16[96,768]{1,0:T(8,128)(2,1)} async-done(((bf16[768,768]{1,0:T(8,128)(2,1)}), bf16[96,768]{1,0:T(8,128)(2,1)}) %reduce-scatter.41.cloned.1.call-update) | async-done | bytes 147472
  831.4 64.5 %reduce-scatter.43.cloned.1.call-done = bf16[96,768]{1,0:T(8,128)(2,1)} async-done(((bf16[768,768]{1,0:T(8,128)(2,1)}), bf16[96,768]{1,0:T(8,128)(2,1)}) %reduce-scatter.43.cloned.1.call-update) | async-done | bytes 147472
  897.7 64.5 %reduce-scatter.25.cloned.1.call-done = bf16[96,768]{1,0:T(8,128)(2,1)} async-done(((bf16[768,768]{1,0:T(8,128)(2,1)}), bf16[96,768]{1,0:T(8,128)(2,1)}) %reduce-scatter.25.cloned.1.call-update) | async-done | bytes 147472 | tf_op jit(solution)/shard_map/reduce_scatter | solution.py:331
  962.2 98.0 %reduce-scatter.27.cloned.1.call-done = bf16[96,3072]{1,0:T(8,128)(2,1)} async-done(((bf16[768,3072]{1,0:T(8,128)(2,1)}), bf16[96,3072]{1,0:T(8,128)(2,1)}) %reduce-scatter.27.cloned.1.call-update) | async-done | bytes 589840 | tf_op jit(solution)/shard_map/reduce_scatter | solution.py:343
  1060.3 98.7 %reduce-scatter.29.cloned.1.call-done = bf16[384,768]{1,0:T(8,128)(2,1)} async-done(((bf16[3072,768]{1,0:T(8,128)(2,1)}), bf16[384,768]{1,0:T(8,128)(2,1)}) %reduce-scatter.29.cloned.1.call-update) | async-done | bytes 589840 | tf_op jit(solution)/shard_map/reduce_scatter | solution.py:349
  1174.0 8.5 all-reduce.19
  1200.1 11.9 all-reduce.23.cloned.1.call-done
  (466 shorter events, 212.3 us)
Async XLA Ops:
  7.2 50.1 %copy-start.110 = (u32[32]{0:T(128)S(1)}, u32[32]{0:T(128)}, u32[]{:S(2)}) copy-start(u32[32]{0:T(128)} %constant.96) | copy-start | bytes 388
  7.2 89.1 %copy-start.14 = (bf16[8,128,768]{2,1,0:T(8,128)(2,1)S(1)}, bf16[8,128,768]{2,1,0:T(8,128)(2,1)}, u32[]{:S(2)}) copy-start(bf16[8,128,768]{2,1,0:T(8,128)(2,1)} %param.18) | copy-start | bytes 4718596
  7.2 51.4 %copy-start.115 = (bf16[96]{0:T(256)(128)(2,1)S(1)}, bf16[96]{0:T(256)(128)(2,1)}, u32[]{:S(2)}) copy-start(bf16[96]{0:T(256)(128)(2,1)} %param.22) | copy-start | bytes 580
  7.2 51.6 %copy-start.116 = (bf16[96]{0:T(256)(128)(2,1)S(1)}, bf16[96]{0:T(256)(128)(2,1)}, u32[]{:S(2)}) copy-start(bf16[96]{0:T(256)(128)(2,1)} %param.25) | copy-start | bytes 580
  7.2 51.9 %copy-start.117 = (bf16[96]{0:T(256)(128)(2,1)S(1)}, bf16[96]{0:T(256)(128)(2,1)}, u32[]{:S(2)}) copy-start(bf16[96]{0:T(256)(128)(2,1)} %param.27) | copy-start | bytes 580
  7.2 52.1 %copy-start.118 = (bf16[96]{0:T(256)(128)(2,1)S(1)}, bf16[96]{0:T(256)(128)(2,1)}, u32[]{:S(2)}) copy-start(bf16[96]{0:T(256)(128)(2,1)} %param.29) | copy-start | bytes 580
  7.3 52.3 %copy-start.119 = (bf16[96]{0:T(256)(128)(2,1)S(1)}, bf16[96]{0:T(256)(128)(2,1)}, u32[]{:S(2)}) copy-start(bf16[96]{0:T(256)(128)(2,1)} %param.28) | copy-start | bytes 580
  7.3 52.5 %copy-start.120 = (bf16[96]{0:T(256)(128)(2,1)S(1)}, bf16[96]{0:T(256)(128)(2,1)}, u32[]{:S(2)}) copy-start(bf16[96]{0:T(256)(128)(2,1)} %param.34) | copy-start | bytes 580
  7.3 52.8 %copy-start.121 = (bf16[96]{0:T(256)(128)(2,1)S(1)}, bf16[96]{0:T(256)(128)(2,1)}, u32[]{:S(2)}) copy-start(bf16[96]{0:T(256)(128)(2,1)} %param.33) | copy-start | bytes 580
  7.3 46.8 %all-gather.18.cloned.1.call-start = ((), (), s32[]{:S(2)}) async-start(), calls=%async_computation.13 | async-start | bytes 1327104 | tf_op jit(solution)/shard_map/all_gather | solution.py:289
  8.0 88.3 %all-gather.12.cloned.1.call-start = ((), (), s32[]{:S(2)}) async-start(), calls=%async_computation.10 | async-start | bytes 1327104 | tf_op jit(solution)/shard_map/all_gather | solution.py:290
  8.8 129.7 %all-gather.16.cloned.1.call-start = ((), (), s32[]{:S(2)}) async-start(), calls=%async_computation.12 | async-start | bytes 1327104 | tf_op jit(solution)/shard_map/all_gather | solution.py:287
  9.5 158.3 %all-gather.30.cloned.1.call-start = ((), (), s32[]{:S(2)}) async-start(), calls=%async_computation.19 | async-start | bytes 3932160 | tf_op jit(solution)/shard_map/all_gather | solution.py:99
  57.3 141.0 %all-gather.28.cloned.1.call-start = ((), (), s32[]{:S(2)}) async-start(), calls=%async_computation.18 | async-start | bytes 3932160 | tf_op jit(solution)/shard_map/all_gather | solution.py:100
  99.3 142.2 %all-gather.22.cloned.1.call-start = ((), (), s32[]{:S(2)}) async-start(), calls=%async_computation.15 | async-start | bytes 1327104 | tf_op jit(solution)/shard_map/all_gather | solution.py:292
  99.9 170.5 %all-gather.20.cloned.1.call-start = ((), (), s32[]{:S(2)}) async-start(), calls=%async_computation.14 | async-start | bytes 3932160 | tf_op jit(solution)/shard_map/all_gather | solution.py:99
  102.9 198.1 %all-gather.14.cloned.1.call-start = ((), (), s32[]{:S(2)}) async-start(), calls=%async_computation.11 | async-start | bytes 3932160 | tf_op jit(solution)/shard_map/all_gather | solution.py:100
  104.7 278.5 %all-gather.24.cloned.1.call-start = ((), (), s32[]{:S(2)}) async-start(), calls=%async_computation.16 | async-start | bytes 5308416 | tf_op jit(solution)/shard_map/all_gather | solution.py:296
  105.4 357.8 %all-gather.26.cloned.1.call-start = ((), (), s32[]{:S(2)}) async-start(), calls=%async_computation.17 | async-start | bytes 5308416 | tf_op jit(solution)/shard_map/all_gather | solution.py:298
  106.0 512.1 %reduce-scatter.35.cloned.1.call-start = ((), (), s32[]{:S(2)}) async-start(), calls=%async_computation.25 | async-start | bytes 3932160
  137.3 332.9 %copy-start.103 = (f32[768]{0:T(1024)}, f32[768]{0:T(1024)S(1)}, u32[]{:S(2)}) copy-start(f32[768]{0:T(1024)S(1)} %convert_element_type.390) | copy-start | bytes 9220
  210.4 33.2 %copy-start.24 = (f32[4,128,12,64]{1,3,2,0:T(8,128)}, f32[4,128,12,64]{1,3,2,0:T(8,128)S(1)}, u32[]{:S(2)}) copy-start(f32[4,128,12,64]{1,3,2,0:T(8,128)S(1)} %bitcast_divide_fusion) | copy-start | bytes 4718596
  210.4 31.0 %copy-start.15 = (bf16[8,128,768]{2,1,0:T(8,128)(2,1)S(1)}, bf16[8,128,768]{2,1,0:T(8,128)(2,1)}, u32[]{:S(2)}) copy-start(bf16[8,128,768]{2,1,0:T(8,128)(2,1)} %param.18) | copy-start | bytes 4718596
  243.7 256.6 %copy-start.82 = (f32[4,128]{1,0:T(4,128)}, f32[4,128]{1,0:T(4,128)S(1)}, u32[]{:S(2)}) copy-start(f32[4,128]{1,0:T(4,128)S(1)} %broadcast_multiply_fusion.9) | copy-start | bytes 6148
  245.1 255.2 %copy-start.97 = (f32[4,128]{1,0:T(4,128)}, f32[4,128]{1,0:T(4,128)S(1)}, u32[]{:S(2)}) copy-start(f32[4,128]{1,0:T(4,128)S(1)} %add_rsqrt_fusion.1) | copy-start | bytes 6148
  315.0 225.5 %copy-start.8 = (f32[4,128,768]{2,1,0:T(8,128)}, f32[4,128,768]{2,1,0:T(8,128)S(1)}, u32[]{:S(2)}) copy-start(f32[4,128,768]{2,1,0:T(8,128)S(1)} %get-tuple-element.157) | copy-start | bytes 4718596
  315.0 225.5 %copy-start.72 = (f32[4,128]{1,0:T(4,128)}, f32[4,128]{1,0:T(4,128)S(1)}, u32[]{:S(2)}) copy-start(f32[4,128]{1,0:T(4,128)S(1)} %broadcast_multiply_fusion.11) | copy-start | bytes 6148
  315.4 225.2 %copy-start.79 = (f32[4,128]{1,0:T(4,128)}, f32[4,128]{1,0:T(4,128)S(1)}, u32[]{:S(2)}) copy-start(f32[4,128]{1,0:T(4,128)S(1)} %add_rsqrt_fusion.3) | copy-start | bytes 6148
  473.0 27.3 %copy-start.12 = (f32[4,128,768]{2,1,0:T(8,128)}, f32[4,128,768]{2,1,0:T(8,128)S(1)}, u32[]{:S(2)}) copy-start(f32[4,128,768]{2,1,0:T(8,128)S(1)} %get-tuple-element.166) | copy-start | bytes 4718596
  537.0 83.9 %reduce-scatter.31.cloned.1.call-start = ((), (), s32[]{:S(2)}) async-start(), calls=%async_computation.23 | async-start | bytes 3932160
  567.7 86.7 %reduce-scatter.33.cloned.1.call-start = ((), (), s32[]{:S(2)}) async-start(), calls=%async_computation.24 | async-start | bytes 3932160
  583.2 111.6 %reduce-scatter.37.cloned.1.call-start = ((), (), s32[]{:S(2)}) async-start(), calls=%async_computation.26 | async-start | bytes 3932160
  599.2 163.6 %reduce-scatter.39.cloned.1.call-start = ((), (), s32[]{:S(2)}) async-start(), calls=%async_computation.27 | async-start | bytes 1327104
  618.0 211.7 %reduce-scatter.41.cloned.1.call-start = ((), (), s32[]{:S(2)}) async-start(), calls=%async_computation.28 | async-start | bytes 1327104
  628.9 267.1 %reduce-scatter.43.cloned.1.call-start = ((), (), s32[]{:S(2)}) async-start(), calls=%async_computation.29 | async-start | bytes 1327104
  657.0 42.9 %copy-start.30 = (bf16[4,128,768]{1,2,0:T(8,128)(2,1)}, bf16[4,128,768]{1,2,0:T(8,128)(2,1)S(1)}, u32[]{:S(2)}) copy-start(bf16[4,128,768]{1,2,0:T(8,128)(2,1)S(1)} %copy.137) | copy-start | bytes 2359300
  704.3 257.9 %reduce-scatter.25.cloned.1.call-start = ((), (), s32[]{:S(2)}) async-start(), calls=%async_computation.20 | async-start | bytes 1327104 | tf_op jit(solution)/shard_map/reduce_scatter | solution.py:331
  708.6 351.6 %reduce-scatter.27.cloned.1.call-start = ((), (), s32[]{:S(2)}) async-start(), calls=%async_computation.21 | async-start | bytes 5308416 | tf_op jit(solution)/shard_map/reduce_scatter | solution.py:343
  718.6 440.4 %reduce-scatter.29.cloned.1.call-start = ((), (), s32[]{:S(2)}) async-start(), calls=%async_computation.22 | async-start | bytes 5308416 | tf_op jit(solution)/shard_map/reduce_scatter | solution.py:349
  729.3 482.7 %all-reduce.23.cloned.1.call-start = ((), (), s32[]{:S(2)}) async-start(), calls=%async_computation.30 | async-start | bytes 3833856 | tf_op jit(solution)/shard_map/psum | solution.py:363
  737.1 68.3 %copy-start.11 = (f32[4,128,768]{2,1,0:T(8,128)S(1)}, f32[4,128,768]{2,1,0:T(8,128)}, u32[]{:S(2)}) copy-start(f32[4,128,768]{2,1,0:T(8,128)} %copy-done.10) | copy-start | bytes 4718596
  737.1 68.3 %copy-start.76 = (f32[4,128]{1,0:T(4,128)S(1)}, f32[4,128]{1,0:T(4,128)}, u32[]{:S(2)}) copy-start(f32[4,128]{1,0:T(4,128)} %copy-done.75) | copy-start | bytes 6148
  737.1 68.3 %copy-start.78 = (f32[4,128]{1,0:T(4,128)S(1)}, f32[4,128]{1,0:T(4,128)}, u32[]{:S(2)}) copy-start(f32[4,128]{1,0:T(4,128)} %copy-done.77) | copy-start | bytes 6148
  1159.0 36.9 %copy-start.31 = (bf16[4,128,768]{1,2,0:T(8,128)(2,1)S(1)}, bf16[4,128,768]{1,2,0:T(8,128)(2,1)}, u32[]{:S(2)}) copy-start(bf16[4,128,768]{1,2,0:T(8,128)(2,1)} %copy-done.30) | copy-start | bytes 2359300
  1159.0 36.9 %copy-start.47 = (bf16[768,768]{1,0:T(8,128)(2,1)S(1)}, bf16[768,768]{1,0:T(8,128)(2,1)}, u32[]{:S(2)}) copy-start(bf16[768,768]{1,0:T(8,128)(2,1)} %all-gather.12.cloned.1.call-done) | copy-start | bytes 3538948
  1159.0 36.9 %copy-start.74 = (f32[4,128]{1,0:T(4,128)S(1)}, f32[4,128]{1,0:T(4,128)}, u32[]{:S(2)}) copy-start(f32[4,128]{1,0:T(4,128)} %copy-done.72) | copy-start | bytes 6148
  1159.1 36.8 %copy-start.81 = (f32[4,128]{1,0:T(4,128)S(1)}, f32[4,128]{1,0:T(4,128)}, u32[]{:S(2)}) copy-start(f32[4,128]{1,0:T(4,128)} %copy-done.79) | copy-start | bytes 6148
  1159.1 36.8 %copy-start.85 = (f32[4,128]{1,0:T(4,128)S(1)}, f32[4,128]{1,0:T(4,128)}, u32[]{:S(2)}) copy-start(f32[4,128]{1,0:T(4,128)} %copy-done.84) | copy-start | bytes 6148
  (104 other events, 553.2 us)
Sparse Core Ops, SparseCore 0:
  10.3 43.7 all-gather.17
  56.3 40.0 all-gather.11
  98.5 39.8 all-gather.15
  140.4 27.2 all-gather.29
  169.8 28.5 all-gather.27
  200.4 41.0 all-gather.21
  243.0 27.2 all-gather.19
  272.5 28.5 all-gather.13
  303.2 79.8 all-gather.23
  385.2 78.0 all-gather.25
  537.1 36.0 reduce-scatter.34
  575.8 37.9 reduce-scatter.30
  616.4 37.9 reduce-scatter.32
  656.9 37.9 reduce-scatter.36
  698.7 64.0 reduce-scatter.38
  766.6 63.0 reduce-scatter.40
  833.0 62.9 reduce-scatter.42
  899.2 62.9 reduce-scatter.24
  965.9 94.3 reduce-scatter.26
  1063.8 95.1 reduce-scatter.28
  1162.4 49.6 all-reduce.22
where the time goes:
time: 1240 us; the launch traced here: 1230 us
  waiting for transfers between devices  707 us (57%)
  matrix products  193 us (16%)
  local copies, waits for them, and re-layouts  125 us (10%)
  blocking collectives  111 us (9%)
  other arithmetic  73.3 us (6%)
  between operations  18.8 us (2%)
    unnamed x28, waiting for transfers between devices  177 us
    reduce_scatter x1, waiting for transfers between devices, local(): lax.psum_scatter(totals[11].astype(jnp.bfloat16), 'dp', scatter_dimension...  98.7 us
    reduce_scatter x1, waiting for transfers between devices, local(): lax.psum_scatter(totals[9].astype(jnp.bfloat16), 'dp', scatter_dimension=...  98 us
    unnamed x314, local copies, waits for them, and re-layouts  94 us
    unnamed x2, blocking collectives  71.3 us
    all_gather x1, waiting for transfers between devices, local(): lax.all_gather(up_weight, 'dp', axis=0, tiled=True)  67.8 us
    reduce_scatter x1, waiting for transfers between devices, local(): lax.psum_scatter(totals[5].astype(jnp.bfloat16), 'dp', scatter_dimension=...  64.5 us
    dot_general x12, matrix products, matmul_back(): jnp.einsum('gok,vk->gov', gradient_bundle, weight_matrix, preferred_eleme...  49.2 us
  transfers between devices with their start and end apart: 21, of which 18 were waited for; matrix products, arithmetic and copies ran while one was open for 23% of the time, Pallas kernels for 0%

commit v1 on v0

v1 whole, which is shorter than its diff:
```python
import jax
import jax.numpy as jnp
from jax import lax
from jax.sharding import PartitionSpec as P

H = 12
DH = 64

EPS = 1e-12
NEG = -1e30
ROOT_HALF = 0.7071067811865476
DENSITY = 0.3989422804014327
BF = jnp.bfloat16
F32 = jnp.float32


def matmul(a, b):
    return lax.dot_general(a, b, (((1,), (0,)), ((), ())), preferred_element_type=F32)


def matmul_back(a, b):
    return lax.dot_general(a, b, (((1,), (1,)), ((), ())), preferred_element_type=F32)


def outer_sum(a, b):
    return lax.dot_general(a, b, (((0,), (0,)), ((), ())), preferred_element_type=F32)


def total(a):
    return jnp.sum(a.astype(F32), axis=0)


def normalize(rows):
    center = rows - jnp.mean(rows, axis=-1, keepdims=True)
    inverse = lax.rsqrt(jnp.mean(center * center, axis=-1, keepdims=True) + EPS)
    return center * inverse, inverse


def normalize_back(grad, normed, inverse):
    return inverse * (
        grad
        - jnp.mean(grad, axis=-1, keepdims=True)
        - normed * jnp.mean(grad * normed, axis=-1, keepdims=True)
    )


class Links:
    def __init__(self):
        self.nd = lax.axis_size("dp")
        self.nb = lax.axis_size("blk")
        self.bits = self.nb.bit_length() - 1
        self.blk = lax.axis_index("blk")
        self.dp = lax.axis_index("dp")
        n = self.nd
        self.order = list(range(0, n, 2)) + list(range(n - 1, 0, -2))
        place = {d: i for i, d in enumerate(self.order)}
        self.core = self.blk & 1
        self.sign = 1 - 2 * self.core
        self.place = jnp.where(
            self.dp % 2 == 0, self.dp // 2, n - 1 - self.dp // 2
        )
        pairs = []
        for d in range(n):
            for b in range(self.nb):
                step = 1 if b % 2 == 0 else -1
                target = self.order[(place[d] + step) % n]
                pairs.append((d * self.nb + b, target * self.nb + b))
        self.pairs = pairs

    def swap(self, a, bit):
        return lax.ppermute(a, "blk", [(i, i ^ (1 << bit)) for i in range(self.nb)])

    def step(self, a):
        return lax.ppermute(a, ("dp", "blk"), self.pairs)

    def shard_at(self, offset):
        n = self.nd
        at = (self.place + offset) % n
        return jnp.where(at < n // 2, 2 * at, 2 * (n - 1 - at) + 1)

    def to_rows(self, a):
        for bit in reversed(range(self.bits)):
            half = a.shape[0] // 2
            mine = (self.blk >> bit) & 1
            keep = lax.dynamic_slice_in_dim(a, mine * half, half, 0)
            send = lax.dynamic_slice_in_dim(a, (1 - mine) * half, half, 0)
            a = jnp.concatenate([keep, self.swap(send, bit)], axis=1)
        return a

    def from_rows(self, a):
        for bit in range(self.bits):
            half = a.shape[1] // 2
            mine = (self.blk >> bit) & 1
            keep, got = a[:, :half], self.swap(a[:, half:], bit)
            a = jnp.where(
                mine == 0,
                jnp.concatenate([keep, got], 0),
                jnp.concatenate([got, keep], 0),
            )
        return a

    def gather(self, piece):
        n, m = self.nd, piece.shape[0]
        held, now = [], piece
        for _ in range(n // 2 - 1):
            now = self.step(now)
            held.append(now)
        far = self.step(lax.dynamic_slice_in_dim(now, self.core * (m // 2), m // 2, 0))
        packed = jnp.concatenate(held + [far], 0)
        other = self.swap(packed, 0)
        whole = jnp.zeros((n,) + piece.shape, piece.dtype)
        put = lambda w, a, at: lax.dynamic_update_slice(
            w, a[None], (at,) + (0,) * a.ndim
        )
        whole = put(whole, piece, self.dp)
        for s in range(1, n // 2):
            whole = put(whole, packed[(s - 1) * m : s * m], self.shard_at(-self.sign * s))
            whole = put(whole, other[(s - 1) * m : s * m], self.shard_at(self.sign * s))
        tops = jnp.where(self.core == 0, packed[-(m // 2) :], other[-(m // 2) :])
        lows = jnp.where(self.core == 0, other[-(m // 2) :], packed[-(m // 2) :])
        return put(whole, jnp.concatenate([tops, lows], 0), self.shard_at(n // 2))

    def scatter(self, parts):
        n, m = self.nd, parts.shape[1]
        parts = parts.astype(BF)
        pick = lambda at: lax.dynamic_index_in_dim(parts, at, 0, keepdims=False)
        halved = lambda a, c: lax.dynamic_slice_in_dim(a, c * (m // 2), m // 2, 0)
        far = pick(self.shard_at(n // 2))
        send = [pick(self.shard_at(-self.sign * s)) for s in range(1, n // 2)]
        send.append(halved(far, 1 - self.core))
        got = self.swap(jnp.concatenate(send, 0), 0).astype(F32)
        acc = halved(far, self.core).astype(F32) + got[-(m // 2) :]
        moved = self.step(acc.astype(BF)).astype(F32)
        zero = jnp.zeros((m // 2,) + moved.shape[1:], F32)
        moved = jnp.where(
            self.core == 0,
            jnp.concatenate([moved, zero], 0),
            jnp.concatenate([zero, moved], 0),
        )
        for s in range(n // 2 - 1, 0, -1):
            acc = pick(self.shard_at(self.sign * s)).astype(F32) + got[(s - 1) * m : s * m] + moved
            moved = self.step(acc.astype(BF)).astype(F32)
        acc = pick(self.dp).astype(F32) + moved
        for bit in range(self.bits):
            low = acc.astype(BF)
            acc = low.astype(F32) + self.swap(low, bit).astype(F32)
        return acc


def local(
    tokens,
    fragments,
    cotangent,
    query_weight,
    query_bias,
    key_weight,
    value_weight,
    value_bias,
    out_weight,
    out_bias,
    first_gain,
    first_shift,
    up_weight,
    up_bias,
    down_weight,
    down_bias,
    second_gain,
    second_shift,
):
    links = Links()
    n = links.nd
    shard, dim = query_weight.shape
    wide = up_bias.shape[0]
    vectors = (
        query_bias,
        value_bias,
        out_bias,
        first_gain,
        first_shift,
        down_bias,
        second_gain,
        second_shift,
        up_bias,
    )
    count = sum(v.shape[0] for v in vectors)
    used = 3 * shard + -(-count // dim)
    rows = -(-used // 32) * 32

    def pack(q, k, v, vecs, dtype):
        flat = jnp.concatenate([x.astype(dtype) for x in vecs], -1)
        room = (rows - 3 * shard) * dim - count
        flat = jnp.pad(flat, [(0, 0)] * (flat.ndim - 1) + [(0, room)])
        flat = flat.reshape(flat.shape[:-1] + (rows - 3 * shard, dim))
        return jnp.concatenate([q.astype(dtype), k.astype(dtype), v.astype(dtype), flat], -2)

    def unpack(a):
        q, k, v = (a[..., i * shard : (i + 1) * shard, :] for i in range(3))
        flat = a[..., 3 * shard :, :].reshape(a.shape[:-2] + (-1,))
        out, at = [], 0
        for x in vectors:
            out.append(flat[..., at : at + x.shape[0]])
            at += x.shape[0]
        return q, k, v, out

    first = links.gather(pack(query_weight, key_weight, value_weight, vectors, BF))
    ids = links.to_rows(fragments)
    x = links.to_rows(tokens)
    count_rows, length = ids.shape
    second_group = links.gather(jnp.concatenate([out_weight, up_weight], 1))
    third = links.gather(down_weight)
    g = links.to_rows(cotangent)

    q_w, k_w, v_w, vecs = unpack(first)
    q_w, k_w, v_w = (w.reshape(dim, dim) for w in (q_w, k_w, v_w))
    q_b, v_b, o_b, gain1, shift1, d_b, gain2, shift2, u_b = (
        v.reshape(-1).astype(F32) for v in vecs
    )
    second_group = second_group.reshape(dim, dim + wide * n)
    o_w, u_w = second_group[:, :dim], second_group[:, dim:]
    d_w = third.reshape(-1, dim)

    x = x.reshape(-1, dim)
    g = g.reshape(-1, dim).astype(F32)
    heads = lambda a: a.reshape(count_rows, length, H, DH).transpose(0, 2, 1, 3)
    merge = lambda a: a.transpose(0, 2, 1, 3).reshape(-1, dim)
    factor = DH**-0.5
    q = (matmul(x, q_w) + q_b).astype(BF)
    k = matmul(x, k_w).astype(BF)
    v = (matmul(x, v_w) + v_b).astype(BF)
    qh, kh, vh = heads(q), heads(k), heads(v)
    allowed = (ids[:, :, None] == ids[:, None, :])[:, None]
    scores = jnp.einsum("rhqd,rhkd->rhqk", qh, kh, preferred_element_type=F32) * factor
    scores = jnp.where(allowed, scores, NEG)
    top = jnp.max(scores, axis=-1, keepdims=True)
    e = jnp.exp(scores - top)
    probs = e / jnp.sum(e, axis=-1, keepdims=True)
    low = probs.astype(BF)
    full = jnp.einsum("rhqk,rhkd->rhqd", low, vh, preferred_element_type=F32)
    attended = merge(full.astype(BF))
    r1 = x.astype(F32) + matmul(attended, o_w) + o_b
    n1, i1 = normalize(r1)
    hidden = n1 * gain1 + shift1
    hidden_low = hidden.astype(BF)
    before = matmul(hidden_low, u_w) + u_b
    phi = 0.5 * (1.0 + lax.erf(before * ROOT_HALF))
    active = (before * phi).astype(BF)
    slope = phi + before * DENSITY * jnp.exp(-0.5 * before * before)
    n2, i2 = normalize(hidden + matmul(active, d_w) + d_b)
    result = (n2 * gain2 + shift2).astype(BF)
    result = links.from_rows(result.reshape(count_rows, length, dim))

    grad_shift2 = total(g)
    grad_gain2 = total(g * n2)
    g_r2 = normalize_back(g * gain2, n2, i2)
    g_second = g_r2.astype(BF)
    grad_down_bias = total(g_second)
    grad_down = outer_sum(active, g_second)
    grad_down = links.scatter(grad_down.reshape(n, -1, dim))
    g_before = (matmul_back(g_second, d_w) * slope).astype(BF)
    grad_up_bias = total(g_before)
    grad_up = outer_sum(hidden_low, g_before)
    g_hidden = g_r2 + matmul_back(g_before, u_w)
    grad_shift1 = total(g_hidden)
    grad_gain1 = total(g_hidden * n1)
    g_r1 = normalize_back(g_hidden * gain1, n1, i1)
    g_branch = g_r1.astype(BF)
    grad_out_bias = total(g_branch)
    grad_out = outer_sum(attended, g_branch)
    both = links.scatter(
        jnp.concatenate([grad_out, grad_up], 1).reshape(n, shard, -1)
    )
    grad_out, grad_up = both[:, :dim], both[:, dim:]
    gh = heads(matmul_back(g_branch, o_w).astype(BF))
    g_v = jnp.einsum("rhqk,rhqd->rhkd", low, gh, preferred_element_type=F32)
    g_p = jnp.einsum("rhqd,rhkd->rhqk", gh, vh, preferred_element_type=F32)
    delta = jnp.sum(probs * g_p, axis=-1, keepdims=True)
    g_s = (probs * (g_p - delta)).astype(BF)
    g_q = jnp.einsum("rhqk,rhkd->rhqd", g_s, kh, preferred_element_type=F32) * factor
    g_k = jnp.einsum("rhqk,rhqd->rhkd", g_s, qh, preferred_element_type=F32) * factor
    g_q, g_k, g_v = (merge(a.astype(BF)) for a in (g_q, g_k, g_v))
    g_x = g_r1 + matmul_back(g_q, q_w) + matmul_back(g_k, k_w) + matmul_back(g_v, v_w)
    g_x = links.from_rows(g_x.astype(BF).reshape(count_rows, length, dim))
    sums = (
        total(g_q),
        total(g_v),
        grad_out_bias,
        grad_gain1,
        grad_shift1,
        grad_down_bias,
        grad_gain2,
        grad_shift2,
        grad_up_bias,
    )
    weights = (outer_sum(x, a).reshape(n, shard, dim) for a in (g_q, g_k, g_v))
    last = links.scatter(pack(*weights, tuple(s.reshape(n, -1) for s in sums), BF))
    grad_q, grad_k, grad_v, vecs = unpack(last)
    (
        grad_q_b,
        grad_v_b,
        grad_out_bias,
        grad_gain1,
        grad_shift1,
        grad_down_bias,
        grad_gain2,
        grad_shift2,
        grad_up_bias,
    ) = vecs
    return (
        result,
        g_x,
        grad_q,
        grad_q_b,
        grad_k,
        grad_v,
        grad_v_b,
        grad_out,
        grad_out_bias,
        grad_gain1,
        grad_shift1,
        grad_up,
        grad_up_bias,
        grad_down,
        grad_down_bias,
        grad_gain2,
        grad_shift2,
    )


def solution(mesh):
    three, two, one = P("dp", "blk", None), P("dp", None), P("dp")
    params = (two, one, two, two, one, two, one, one, one, two, one, two, one, one, one)
    return jax.shard_map(
        local,
        mesh=mesh,
        in_specs=(three, P("dp", "blk"), three) + params,
        out_specs=(three, three) + params,
        check_vma=False,
    )
```

time: 1240 us -> 497 us (0.40)
  waiting for transfers between devices: 707 us -> 101 us
  blocking collectives: 111 us -> 0 us
  starting transfers between devices: 1.89 us -> 51.3 us
  matrix products: 193 us -> 160 us
  between operations: 18.8 us -> 2.27 us
  local copies, waits for them, and re-layouts: 125 us -> 112 us
    reduce_scatter x3 -> x0, waiting for transfers between devices: 261 us -> none  [the longest x1 98.7 us: local(): lax.psum_scatter(totals[11].astype(jnp.bfloat16), 'dp', scatter_dimension...]
    all_gather x10 -> x0, waiting for transfers between devices: 257 us -> none  [the longest x1 67.8 us: local(): lax.all_gather(up_weight, 'dp', axis=0, tiled=True)]
    unnamed x28 -> x0, waiting for transfers between devices: 177 us -> none
    ppermute x0 -> x46, waiting for transfers between devices: none -> 101 us  [the longest x24 63.8 us: step(): return lax.ppermute(a, ('dp', 'blk'), self.pairs)]
    unnamed x314 -> x130, local copies, waits for them, and re-layouts: 94 us -> 14.3 us
    unnamed x2 -> x0, blocking collectives: 71.3 us -> none
    ppermute x0 -> x46, starting transfers between devices: none -> 51.3 us  [the longest x24 39 us: step(): return lax.ppermute(a, ('dp', 'blk'), self.pairs)]
    dot_general x48 -> x23, matrix products: 193 us -> 144 us  [the longest x6 30.6 us: matmul(): lax.dot_general(a, b, (((1,), (0,)), ((), ())), preferred_element_type=F32)]
  transfers between devices with their start and end apart: 21 -> 46, of which waited for: 18 -> 21; matrix products, arithmetic and copies ran while one was open for 23% -> 33% of each run, Pallas kernels for 0% -> 0%
where the time goes in v1:
time: 497 us; the launch traced here: 491 us
  matrix products  160 us (32%)
  local copies, waits for them, and re-layouts  112 us (23%)
  waiting for transfers between devices  101 us (20%)
  other arithmetic  64.8 us (13%)
  starting transfers between devices  51.3 us (10%)
    ppermute x24, waiting for transfers between devices, step(): return lax.ppermute(a, ('dp', 'blk'), self.pairs)  63.8 us
    ppermute x24, starting transfers between devices, step(): return lax.ppermute(a, ('dp', 'blk'), self.pairs)  39 us
    ppermute x22, waiting for transfers between devices, swap(): return lax.ppermute(a, 'blk', [(i, i ^ 1 << bit) for i in range(self.nb)])  36.9 us
    dot_general x6, matrix products, matmul(): lax.dot_general(a, b, (((1,), (0,)), ((), ())), preferred_element_type=F32)  30.6 us
    dot_general x6, matrix products, matmul_back(): lax.dot_general(a, b, (((1,), (1,)), ((), ())), preferred_element_type=F32)  28.4 us
    dot_general x6, matrix products, outer_sum(): lax.dot_general(a, b, (((0,), (0,)), ((), ())), preferred_element_type=F32)  26.3 us
    dynamic_update_slice x21, local copies, waits for them, and re-layouts, gather(): lax.dynamic_update_slice(w, a[None], (at,) + (0,) * a.ndim)  25.2 us
    convert_element_type x1, other arithmetic, local(): g_s = (probs * (g_p - delta)).astype(BF)  21.3 us
  transfers between devices with their start and end apart: 46, of which 21 were waited for; matrix products, arithmetic and copies ran while one was open for 33% of the time, Pallas kernels for 0%

profile of v1, /device:TPU:0, one launch (start us, length us, event | category | flops | bytes accessed | tf_op | source)
XLA Modules:
  0.0 490.6 jit_solution(11451105794374717147)
XLA Ops:
  1.4 3.0 collective-permute-start.2
  4.4 6.1 %concatenate.110 = bf16[1152]{0:T(1024)(128)(2,1)S(1)} concatenate(bf16[96]{0:T(256)(128)(2,1)} %param.22, bf16[96]{0:T(256)(128)(2,1)} %param.25, bf16[96]{0:T(256)(128)(2,1)} %param.27, bf16[96]{0:T(256)(128)(2,1)} %param.28, bf16[96]{0:T(256)(128)(2,1)} %param.29, bf16[96]{0:T(256)(128)(2,1)} %param.33, bf16[96]{0:T(256)(128)(2,1)} %param.34, bf16[96]{0:T(256)(128)(2,1)} %param.35, ...), dimensions={0} | concatenate | bytes 4608 | tf_op jit(solution)/shard_map/concatenate | solution.py:190
  38.2 3.7 collective-permute-done.5
  47.8 7.3 %collective-permute-done.6 = bf16[320,768]{1,0:T(8,128)(2,1)S(1)} collective-permute-done((bf16[320,768]{1,0:T(8,128)(2,1)S(1)}, bf16[320,768]{1,0:T(8,128)(2,1)S(1)}, u32[]{:S(2)}, u32[]{:S(2)}) %collective-permute-start.6) | collective-permute-done | bytes 491552 | tf_op jit(solution)/shard_map/ppermute | solution.py:74
  67.9 3.3 collective-permute-done.16
  73.6 5.6 %collective-permute-done.11 = bf16[96,3840]{1,0:T(8,128)(2,1)S(1)} collective-permute-done((bf16[96,3840]{1,0:T(8,128)(2,1)S(1)}, bf16[96,3840]{1,0:T(8,128)(2,1)S(1)}, u32[]{:S(2)}, u32[]{:S(2)}) %collective-permute-start.11) | collective-permute-done | bytes 737312 | tf_op jit(solution)/shard_map/ppermute | solution.py:74
  84.9 3.1 pad_maximum_fusion.4
  100.1 3.9 fusion.136
  105.3 3.8 add_convert_fusion.3
  109.1 2.6 copy.47
  111.7 3.9 reshape.298
  115.5 3.8 add_convert_fusion.2
  119.3 2.6 copy.51
  121.9 3.8 reshape.302
  125.8 3.8 convolution_convert_fusion.3
  129.6 2.6 copy.48
  132.1 2.9 reshape.300
  135.0 15.5 %fusion.143 = (f32[2,12,512]{2,1,0:T(8,128)}, f32[2,12,512,512]{2,3,1,0:T(8,128)}) fusion(pred[2,512,512]{1,2,0:T(8,128)(4,1)} %broadcast_compare_fusion, bf16[2,12,512,64]{2,0,3,1:T(2,128)(2,1)S(1)} %bitcast.269, bf16[2,12,512,64]{2,0,3,1:T(2,128)(2,1)} %bitcast.308), kind=kOutput, calls=%fused_computation.274 | convolution fusion | flops 830472704 | bytes 28884992 | tf_op jit(solution)/shard_map/sub | solution.py:235
  150.6 11.0 %fusion.55 = bf16[2,512,12,64]{1,3,2,0:T(8,128)(2,1)S(1)} fusion(bf16[2,12,512,64]{2,0,3,1:T(2,128)(2,1)} %bitcast.310, f32[2,12,512,512]{2,3,1,0:T(8,128)} %get-tuple-element.87, f32[2,12,512]{2,1,0:T(8,128)} %get-tuple-element.86), kind=kOutput, calls=%fused_computation.95 | convolution fusion | flops 818675712 | bytes 28360704 | tf_op jit(solution)/shard_map/rhqk,rhkd->rhqd/dot_general | solution.py:238
  182.9 9.7 %multiply_convert_fusion.1 = (bf16[1024,3072]{1,0:T(8,128)(2,1)}, f32[1024,3072]{1,0:T(8,128)}) fusion(f32[3072]{0:T(1024)S(1)} %copy-done.47, bf16[768,3840]{1,0:T(8,128)(2,1)S(1)} %bitcast.287, f32[1024,768]{1,0:T(8,128)S(1)} %get-tuple-element.89, f32[768]{0:T(1024)S(1)} %reshape.318, f32[768]{0:T(1024)S(1)} %reshape.317, f32[1024]{0:T(1024)S(1)} %add_rsqrt_fusion.1, ...), kind=kOutput, calls=%fused_computation.12 | convolution fusion | flops 4854644736 | bytes 26767360 | tf_op jit(solution)/shard_map/dot_general | solution.py:18
  192.6 7.8 %fusion.153 = (f32[1024]{0:T(1024)S(1)}, f32[1024,768]{1,0:T(8,128)S(1)}) fusion(f32[768]{0:T(1024)S(1)} %reshape.320, bf16[1024,3072]{1,0:T(8,128)(2,1)} %get-tuple-element.90, bf16[3072,768]{1,0:T(8,128)(2,1)S(1)} %bitcast.292, f32[768]{0:T(1024)S(1)} %reshape.318, f32[768]{0:T(1024)S(1)} %reshape.317, f32[1024]{0:T(1024)S(1)} %add_rsqrt_fusion.1, ...), kind=kOutput, calls=%fused_computation.276 | convolution fusion | flops 4837342208 | bytes 17323008 | tf_op jit(solution)/shard_map/dot_general | solution.py:18
  201.0 2.8 fusion.26
  205.3 7.1 %convolution_convert_fusion = bf16[3072,768]{1,0:T(8,128)(2,1)} fusion(bf16[1024,3072]{1,0:T(8,128)(2,1)S(1)} %bitcast.330, f32[1024,768]{1,0:T(8,128)S(1)} %get-tuple-element.26), kind=kOutput, calls=%fused_computation.23 | convolution fusion | flops 4834983936 | bytes 14155776 | tf_op jit(solution)/shard_map/dot_general | solution.py:26
  212.4 13.1 %fusion.156 = (bf16[3072]{0:T(1024)(128)(2,1)S(1)}, bf16[1024,3072]{1,0:T(8,128)(2,1)}) fusion(f32[1024,3072]{1,0:T(8,128)} %get-tuple-element.91, f32[3072]{0:T(1024)S(1)} %copy-done.47, bf16[3072,768]{1,0:T(8,128)(2,1)S(1)} %bitcast.293, f32[1024,768]{1,0:T(8,128)S(1)} %get-tuple-element.26), kind=kOutput, calls=%fused_computation.279 | convolution fusion | flops 4870370304 | bytes 26757120 | tf_op jit(solution)/shard_map/dot_general | solution.py:22
  225.5 8.1 %multiply_reduce_fusion.1 = (bf16[768]{0:T(1024)(128)(2,1)S(1)}, f32[1024]{0:T(1024)S(1)}, f32[1024]{0:T(1024)S(1)}, bf16[768]{0:T(1024)(128)(2,1)S(1)}, f32[1024,768]{1,0:T(8,128)S(1)}) fusion(f32[1024,768]{1,0:T(8,128)S(1)} %get-tuple-element.89, f32[1024]{0:T(1024)S(1)} %add_rsqrt_fusion.1, f32[1024]{0:T(1024)S(1)} %broadcast_multiply_fusion.4, ...), kind=kOutput, calls=%fused_computation.41 | convolution fusion | flops 4839698432 | bytes 20470784 | tf_op jit(solution)/shard_map/dot_general | solution.py:22
  233.6 10.3 %convolution_convert_fusion.1 = bf16[768,3072]{1,0:T(8,128)(2,1)} fusion(bf16[1024,3072]{1,0:T(8,128)(2,1)} %get-tuple-element.102, f32[1024,768]{1,0:T(8,128)S(1)} %get-tuple-element.89, f32[768]{0:T(1024)S(1)} %reshape.318, f32[768]{0:T(1024)S(1)} %reshape.317, f32[1024]{0:T(1024)S(1)} %add_rsqrt_fusion.1, f32[1024]{0:T(1024)S(1)} %broadcast_multiply_fusion.4), kind=kOutput, calls=%fused_computation.24 | convolution fusion | flops 4838129664 | bytes 14170112 | tf_op jit(solution)/shard_map/dot_general | solution.py:26
  245.1 2.6 convolution_convert_fusion.2
  250.2 2.6 copy.55
  252.8 3.9 reshape.307
  256.7 11.9 %fusion.155 = (bf16[12,64]{1,0:T(8,128)(2,1)S(1)}, bf16[2,512,12,64]{1,3,2,0:T(8,128)(2,1)}) fusion(bf16[2,12,512,64]{2,0,3,1:T(2,128)(2,1)} %bitcast.318, f32[2,12,512,512]{2,3,1,0:T(8,128)} %get-tuple-element.87, f32[2,12,512]{2,1,0:T(8,128)S(1)} %copy-done.46), kind=kOutput, calls=%fused_computation.278 | convolution fusion | flops 819461376 | bytes 28362240 | tf_op jit(solution)/shard_map/rhqk,rhqd->rhkd/dot_general | solution.py:274
  268.6 17.7 %multiply_reduce_fusion = (f32[2,12,512]{2,1,0:T(8,128)S(1)}, f32[2,12,512,512]{2,3,1,0:T(8,128)}) fusion(f32[2,12,512,512]{2,3,1,0:T(8,128)} %get-tuple-element.87, f32[2,12,512]{2,1,0:T(8,128)S(1)} %copy-done.46, bf16[2,12,512,64]{2,0,3,1:T(2,128)(2,1)} %bitcast.311, bf16[2,12,512,64]{2,0,3,1:T(2,128)(2,1)} %bitcast.319), kind=kOutput, calls=%fused_computation.2 | convolution fusion | flops 824168448 | bytes 53575680 | tf_op jit(solution)/shard_map/rhqd,rhkd->rhqk/dot_general | solution.py:275
  286.2 21.3 %multiply_convert_fusion = bf16[2,12,512,512]{2,3,1,0:T(8,128)(2,1)} fusion(f32[2,12,512,512]{2,3,1,0:T(8,128)} %get-tuple-element.96, f32[2,12,512]{2,1,0:T(8,128)S(1)} %get-tuple-element.95, f32[2,12,512,512]{2,3,1,0:T(8,128)} %get-tuple-element.87, f32[2,12,512]{2,1,0:T(8,128)S(1)} %copy-done.46), kind=kLoop, calls=%fused_computation.1 | loop fusion | flops 25165824 | bytes 63012864 | tf_op jit(solution)/shard_map/convert_element_type | solution.py:277
  307.6 10.0 %fusion.59 = bf16[2,512,12,64]{1,3,2,0:T(8,128)(2,1)} fusion(bf16[2,12,512,512]{2,3,1,0:T(8,128)(2,1)} %multiply_convert_fusion, bf16[2,12,512,64]{2,0,3,1:T(2,128)(2,1)} %bitcast.309), kind=kOutput, calls=%fused_computation.97 | convolution fusion | flops 806879232 | bytes 15728640 | tf_op jit(solution)/shard_map/rhqk,rhqd->rhkd/dot_general | solution.py:279
  317.6 8.4 %fusion.154 = (bf16[12,64]{1,0:T(8,128)(2,1)S(1)}, bf16[2,512,12,64]{1,3,2,0:T(8,128)(2,1)}) fusion(bf16[2,12,512,512]{2,3,1,0:T(8,128)(2,1)} %multiply_convert_fusion, bf16[2,12,512,64]{2,0,3,1:T(2,128)(2,1)} %bitcast.270), kind=kOutput, calls=%fused_computation.277 | convolution fusion | flops 807664896 | bytes 15730176 | tf_op jit(solution)/shard_map/rhqk,rhkd->rhqd/dot_general | solution.py:278
  328.9 2.9 dynamic-slice_bitcast_fusion.5
  331.7 2.7 pad_maximum_fusion
  338.2 3.2 copy.66
  347.0 3.0 copy.63
  351.9 3.5 fusion.49
  397.5 3.4 collective-permute-done.28
  402.7 6.1 %collective-permute-done.34 = bf16[96,3840]{1,0:T(8,128)(2,1)S(1)} collective-permute-done((bf16[96,3840]{1,0:T(8,128)(2,1)S(1)}, bf16[96,3840]{1,0:T(8,128)(2,1)S(1)}, u32[]{:S(2)}, u32[]{:S(2)}) %collective-permute-start.34) | collective-permute-done | bytes 737312 | tf_op jit(solution)/shard_map/ppermute | solution.py:74
  411.3 9.0 %collective-permute-done.29 = bf16[320,768]{1,0:T(8,128)(2,1)S(1)} collective-permute-done((bf16[320,768]{1,0:T(8,128)(2,1)S(1)}, bf16[320,768]{1,0:T(8,128)(2,1)S(1)}, u32[]{:S(2)}, u32[]{:S(2)}) %collective-permute-start.29) | collective-permute-done | bytes 491552 | tf_op jit(solution)/shard_map/ppermute | solution.py:74
  422.5 5.8 %collective-permute-done.35 = bf16[96,3840]{1,0:T(8,128)(2,1)S(1)} collective-permute-done((bf16[96,3840]{1,0:T(8,128)(2,1)S(1)}, bf16[96,3840]{1,0:T(8,128)(2,1)S(1)}, u32[]{:S(2)}, u32[]{:S(2)}) %collective-permute-start.35) | collective-permute-done | bytes 737312 | tf_op jit(solution)/shard_map/ppermute | solution.py:74
  434.8 7.6 %collective-permute-done.36 = bf16[96,3840]{1,0:T(8,128)(2,1)S(1)} collective-permute-done((bf16[96,3840]{1,0:T(8,128)(2,1)S(1)}, bf16[96,3840]{1,0:T(8,128)(2,1)S(1)}, u32[]{:S(2)}, u32[]{:S(2)}) %collective-permute-start.36) | collective-permute-done | bytes 737312 | tf_op jit(solution)/shard_map/ppermute | solution.py:74
  444.1 6.9 %collective-permute-done.24 = bf16[4,128,768]{2,1,0:T(8,128)(2,1)S(1)} collective-permute-done((bf16[4,128,768]{2,1,0:T(8,128)(2,1)S(1)}, bf16[4,128,768]{2,1,0:T(8,128)(2,1)S(1)}, u32[]{:S(2)}, u32[]{:S(2)}) %collective-permute-start.24) | collective-permute-done | bytes 786464 | tf_op jit(solution)/shard_map/ppermute | solution.py:71
  452.4 5.9 %collective-permute-done.31 = bf16[320,768]{1,0:T(8,128)(2,1)S(1)} collective-permute-done((bf16[320,768]{1,0:T(8,128)(2,1)S(1)}, bf16[320,768]{1,0:T(8,128)(2,1)S(1)}, u32[]{:S(2)}, u32[]{:S(2)}) %collective-permute-start.31) | collective-permute-done | bytes 491552 | tf_op jit(solution)/shard_map/ppermute | solution.py:71
  464.2 12.5 %collective-permute-done.45 = bf16[384,768]{1,0:T(8,128)(2,1)S(1)} collective-permute-done((bf16[384,768]{1,0:T(8,128)(2,1)S(1)}, bf16[384,768]{1,0:T(8,128)(2,1)S(1)}, u32[]{:S(2)}, u32[]{:S(2)}) %collective-permute-start.45) | collective-permute-done | bytes 589856 | tf_op jit(solution)/shard_map/ppermute | solution.py:71
  477.8 10.5 %collective-permute-done.38 = bf16[96,3840]{1,0:T(8,128)(2,1)S(1)} collective-permute-done((bf16[96,3840]{1,0:T(8,128)(2,1)S(1)}, bf16[96,3840]{1,0:T(8,128)(2,1)S(1)}, u32[]{:S(2)}, u32[]{:S(2)}) %collective-permute-start.38) | collective-permute-done | bytes 737312 | tf_op jit(solution)/shard_map/ppermute | solution.py:71
  (359 shorter events, 175.8 us)
Async XLA Ops:
  1.4 31.5 %collective-permute-start.2 = (s32[4,128]{1,0:T(4,128)S(1)}, s32[4,128]{1,0:T(4,128)S(1)}, u32[]{:S(2)}, u32[]{:S(2)}) collective-permute-start(s32[4,128]{1,0:T(4,128)S(1)} %get-tuple-element.84), channel_id=1, source_target_pairs={{0,2},{1,3},{2,0},{3,1},{4,6},{5,7},{6,4},{7,5},{8,10},{9,11},{10,... | collective-permute-start | bytes 6152 | tf_op jit(solution)/shard_map/ppermute | solution.py:71
  13.5 16.9 %collective-permute-start.4 = (bf16[320,768]{1,0:T(8,128)(2,1)S(1)}, bf16[320,768]{1,0:T(8,128)(2,1)}, u32[]{:S(2)}, u32[]{:S(2)}) collective-permute-start(bf16[320,768]{1,0:T(8,128)(2,1)S(1)} %constant_dynamic-update-slice_fusion), channel_id=1, source_target_pairs={{0,8},{1,5},{2,10},{3,7},{4,0},{5,13},{6,2},{7,15},{8,16},{9,1},{1... | collective-permute-start | bytes 1474568 | tf_op jit(solution)/shard_map/ppermute | solution.py:74
  15.1 30.2 %collective-permute-start.14 = (bf16[384,768]{1,0:T(8,128)(2,1)}, bf16[384,768]{1,0:T(8,128)(2,1)S(1)}, u32[]{:S(2)}, u32[]{:S(2)}) collective-permute-start(bf16[384,768]{1,0:T(8,128)(2,1)} %param.32), channel_id=1, source_target_pairs={{0,8},{1,5},{2,10},{3,7},{4,0},{5,13},{6,2},{7,15},{8,16},{9,1},{1... | collective-permute-start | bytes 1769480 | tf_op jit(solution)/shard_map/ppermute | solution.py:74
  20.2 16.6 %collective-permute-start.9 = (bf16[96,3840]{1,0:T(8,128)(2,1)}, bf16[96,3840]{1,0:T(8,128)(2,1)S(1)}, u32[]{:S(2)}, u32[]{:S(2)}) collective-permute-start(bf16[96,3840]{1,0:T(8,128)(2,1)} %constant_dynamic-update-slice_fusion.4), channel_id=1, source_target_pairs={{0,8},{1,5},{2,10},{3,7},{4,0},{5,13},{6,2},{7,15},{8,16},{9,1},{1... | collective-permute-start | bytes 2211848 | tf_op jit(solution)/shard_map/ppermute | solution.py:74
  22.8 33.9 %collective-permute-start = (bf16[4,128,768]{2,1,0:T(8,128)(2,1)}, bf16[4,128,768]{2,1,0:T(8,128)(2,1)}, u32[]{:S(2)}, u32[]{:S(2)}) collective-permute-start(bf16[4,128,768]{2,1,0:T(8,128)(2,1)} %get-tuple-element.61), channel_id=1, source_target_pairs={{0,2},{1,3},{2,0},{3,1},{4,6},{5,7},{6,4},{7,5},{8,10},{9,11},{10,... | collective-permute-start | bytes 2359304 | tf_op jit(solution)/shard_map/ppermute | solution.py:71
  30.4 11.5 %collective-permute-start.5 = (bf16[320,768]{1,0:T(8,128)(2,1)}, bf16[320,768]{1,0:T(8,128)(2,1)S(1)}, u32[]{:S(2)}, u32[]{:S(2)}) collective-permute-start(bf16[320,768]{1,0:T(8,128)(2,1)} %collective-permute-done.4), channel_id=1, source_target_pairs={{0,8},{1,5},{2,10},{3,7},{4,0},{5,13},{6,2},{7,15},{8,16},{9,1},{1... | collective-permute-start | bytes 1474568 | tf_op jit(solution)/shard_map/ppermute | solution.py:74
  32.9 1.2 collective-permute-start.3
  34.1 23.9 %collective-permute-start.21 = (bf16[4,128,768]{2,1,0:T(8,128)(2,1)}, bf16[4,128,768]{2,1,0:T(8,128)(2,1)S(1)}, u32[]{:S(2)}, u32[]{:S(2)}) collective-permute-start(bf16[4,128,768]{2,1,0:T(8,128)(2,1)} %get-tuple-element.53), channel_id=1, source_target_pairs={{0,2},{1,3},{2,0},{3,1},{4,6},{5,7},{6,4},{7,5},{8,10},{9,11},{10,... | collective-permute-start | bytes 2359304 | tf_op jit(solution)/shard_map/ppermute | solution.py:71
  36.8 30.2 %copy-start.21 = (bf16[96,3840]{1,0:T(8,128)(2,1)}, bf16[96,3840]{1,0:T(8,128)(2,1)S(1)}, u32[]{:S(2)}) copy-start(bf16[96,3840]{1,0:T(8,128)(2,1)S(1)} %collective-permute-done.9) | copy-start | bytes 2211844
  36.8 26.1 %collective-permute-start.10 = (bf16[96,3840]{1,0:T(8,128)(2,1)S(1)}, bf16[96,3840]{1,0:T(8,128)(2,1)S(1)}, u32[]{:S(2)}, u32[]{:S(2)}) collective-permute-start(bf16[96,3840]{1,0:T(8,128)(2,1)S(1)} %collective-permute-done.9), channel_id=1, source_target_pairs={{0,8},{1,5},{2,10},{3,7},{4,0},{5,13},{6,2},{7,15},{8,16},{9,1},{1... | collective-permute-start | bytes 2211848 | tf_op jit(solution)/shard_map/ppermute | solution.py:74
  41.9 13.2 %collective-permute-start.6 = (bf16[320,768]{1,0:T(8,128)(2,1)S(1)}, bf16[320,768]{1,0:T(8,128)(2,1)S(1)}, u32[]{:S(2)}, u32[]{:S(2)}) collective-permute-start(bf16[320,768]{1,0:T(8,128)(2,1)S(1)} %collective-permute-done.5), channel_id=1, source_target_pairs={{0,8},{1,5},{2,10},{3,7},{4,0},{5,13},{6,2},{7,15},{8,16},{9,1},{1... | collective-permute-start | bytes 1474568 | tf_op jit(solution)/shard_map/ppermute | solution.py:74
  45.3 16.0 %collective-permute-start.15 = (bf16[384,768]{1,0:T(8,128)(2,1)S(1)}, bf16[384,768]{1,0:T(8,128)(2,1)S(1)}, u32[]{:S(2)}, u32[]{:S(2)}) collective-permute-start(bf16[384,768]{1,0:T(8,128)(2,1)S(1)} %collective-permute-done.14), channel_id=1, source_target_pairs={{0,8},{1,5},{2,10},{3,7},{4,0},{5,13},{6,2},{7,15},{8,16},{9,1},{1... | collective-permute-start | bytes 1769480 | tf_op jit(solution)/shard_map/ppermute | solution.py:74
  55.1 9.5 %collective-permute-start.7 = (bf16[160,768]{1,0:T(8,128)(2,1)S(1)}, bf16[160,768]{1,0:T(8,128)(2,1)S(1)}, u32[]{:S(2)}, u32[]{:S(2)}) collective-permute-start(bf16[160,768]{1,0:T(8,128)(2,1)S(1)} %constant_dynamic-slice_fusion.4), channel_id=1, source_target_pairs={{0,8},{1,5},{2,10},{3,7},{4,0},{5,13},{6,2},{7,15},{8,16},{9,1},{1... | collective-permute-start | bytes 737288 | tf_op jit(solution)/shard_map/ppermute | solution.py:74
  57.9 24.1 %collective-permute-start.1 = (bf16[2,256,768]{2,1,0:T(8,128)(2,1)S(1)}, bf16[2,256,768]{2,1,0:T(8,128)(2,1)S(1)}, u32[]{:S(2)}, u32[]{:S(2)}) collective-permute-start(bf16[2,256,768]{2,1,0:T(8,128)(2,1)S(1)} %get-tuple-element.60), channel_id=1, source_target_pairs={{0,1},{1,0},{2,3},{3,2},{4,5},{5,4},{6,7},{7,6},{8,9},{9,8},{10,11... | collective-permute-start | bytes 2359304 | tf_op jit(solution)/shard_map/ppermute | solution.py:71
  58.2 24.0 %collective-permute-start.22 = (bf16[2,256,768]{2,1,0:T(8,128)(2,1)S(1)}, bf16[2,256,768]{2,1,0:T(8,128)(2,1)S(1)}, u32[]{:S(2)}, u32[]{:S(2)}) collective-permute-start(bf16[2,256,768]{2,1,0:T(8,128)(2,1)S(1)} %get-tuple-element.52), channel_id=1, source_target_pairs={{0,1},{1,0},{2,3},{3,2},{4,5},{5,4},{6,7},{7,6},{8,9},{9,8},{10,11... | collective-permute-start | bytes 2359304 | tf_op jit(solution)/shard_map/ppermute | solution.py:71
  61.4 9.9 %collective-permute-start.16 = (bf16[384,768]{1,0:T(8,128)(2,1)S(1)}, bf16[384,768]{1,0:T(8,128)(2,1)S(1)}, u32[]{:S(2)}, u32[]{:S(2)}) collective-permute-start(bf16[384,768]{1,0:T(8,128)(2,1)S(1)} %collective-permute-done.15), channel_id=1, source_target_pairs={{0,8},{1,5},{2,10},{3,7},{4,0},{5,13},{6,2},{7,15},{8,16},{9,1},{1... | collective-permute-start | bytes 1769480 | tf_op jit(solution)/shard_map/ppermute | solution.py:74
  63.0 16.2 %collective-permute-start.11 = (bf16[96,3840]{1,0:T(8,128)(2,1)S(1)}, bf16[96,3840]{1,0:T(8,128)(2,1)S(1)}, u32[]{:S(2)}, u32[]{:S(2)}) collective-permute-start(bf16[96,3840]{1,0:T(8,128)(2,1)S(1)} %collective-permute-done.10), channel_id=1, source_target_pairs={{0,8},{1,5},{2,10},{3,7},{4,0},{5,13},{6,2},{7,15},{8,16},{9,1},{1... | collective-permute-start | bytes 2211848 | tf_op jit(solution)/shard_map/ppermute | solution.py:74
  67.0 23.1 %collective-permute-start.8 = (bf16[1120,768]{1,0:T(8,128)(2,1)}, bf16[1120,768]{1,0:T(8,128)(2,1)}, u32[]{:S(2)}, u32[]{:S(2)}) collective-permute-start(bf16[1120,768]{1,0:T(8,128)(2,1)} %pad_maximum_fusion.6), channel_id=1, source_target_pairs={{0,1},{1,0},{2,3},{3,2},{4,5},{5,4},{6,7},{7,6},{8,9},{9,8},{10,11... | collective-permute-start | bytes 5160968 | tf_op jit(solution)/shard_map/ppermute | solution.py:71
  72.0 12.9 %collective-permute-start.17 = (bf16[192,768]{1,0:T(8,128)(2,1)}, bf16[192,768]{1,0:T(8,128)(2,1)}, u32[]{:S(2)}, u32[]{:S(2)}) collective-permute-start(bf16[192,768]{1,0:T(8,128)(2,1)} %constant_dynamic-slice_fusion.2), channel_id=1, source_target_pairs={{0,8},{1,5},{2,10},{3,7},{4,0},{5,13},{6,2},{7,15},{8,16},{9,1},{1... | collective-permute-start | bytes 884744 | tf_op jit(solution)/shard_map/ppermute | solution.py:74
  80.0 8.2 %collective-permute-start.12 = (bf16[48,3840]{1,0:T(8,128)(2,1)}, bf16[48,3840]{1,0:T(8,128)(2,1)S(1)}, u32[]{:S(2)}, u32[]{:S(2)}) collective-permute-start(bf16[48,3840]{1,0:T(8,128)(2,1)} %constant_dynamic-slice_fusion.3), channel_id=1, source_target_pairs={{0,8},{1,5},{2,10},{3,7},{4,0},{5,13},{6,2},{7,15},{8,16},{9,1},{1... | collective-permute-start | bytes 1105928 | tf_op jit(solution)/shard_map/ppermute | solution.py:74
  82.2 43.6 %copy-start.3 = (bf16[2,512,768]{2,1,0:T(8,128)(2,1)}, bf16[2,512,768]{2,1,0:T(8,128)(2,1)S(1)}, u32[]{:S(2)}) copy-start(bf16[2,512,768]{2,1,0:T(8,128)(2,1)S(1)} %pad_maximum_fusion.8) | copy-start | bytes 4718596
  88.0 77.8 %collective-permute-start.18 = (bf16[1344,768]{1,0:T(8,128)(2,1)}, bf16[1344,768]{1,0:T(8,128)(2,1)}, u32[]{:S(2)}, u32[]{:S(2)}) collective-permute-start(bf16[1344,768]{1,0:T(8,128)(2,1)} %pad_maximum_fusion.4), channel_id=1, source_target_pairs={{0,1},{1,0},{2,3},{3,2},{4,5},{5,4},{6,7},{7,6},{8,9},{9,8},{10,11... | collective-permute-start | bytes 6193160 | tf_op jit(solution)/shard_map/ppermute | solution.py:71
  89.8 85.7 %collective-permute-start.13 = (bf16[336,3840]{1,0:T(8,128)(2,1)}, bf16[336,3840]{1,0:T(8,128)(2,1)}, u32[]{:S(2)}, u32[]{:S(2)}) collective-permute-start(bf16[336,3840]{1,0:T(8,128)(2,1)} %pad_maximum_fusion.2), channel_id=1, source_target_pairs={{0,1},{1,0},{2,3},{3,2},{4,5},{5,4},{6,7},{7,6},{8,9},{9,8},{10,11... | collective-permute-start | bytes 7741448 | tf_op jit(solution)/shard_map/ppermute | solution.py:71
  344.5 25.9 %collective-permute-start.39 = (bf16[1344,768]{1,0:T(8,128)(2,1)}, bf16[1344,768]{1,0:T(8,128)(2,1)}, u32[]{:S(2)}, u32[]{:S(2)}) collective-permute-start(bf16[1344,768]{1,0:T(8,128)(2,1)} %pad_maximum_fusion.5), channel_id=1, source_target_pairs={{0,1},{1,0},{2,3},{3,2},{4,5},{5,4},{6,7},{7,6},{8,9},{9,8},{10,11... | collective-permute-start | bytes 6193160 | tf_op jit(solution)/shard_map/ppermute | solution.py:71
  346.6 32.7 %collective-permute-start.32 = (bf16[336,3840]{1,0:T(8,128)(2,1)}, bf16[336,3840]{1,0:T(8,128)(2,1)}, u32[]{:S(2)}, u32[]{:S(2)}) collective-permute-start(bf16[336,3840]{1,0:T(8,128)(2,1)} %pad_maximum_fusion.3), channel_id=1, source_target_pairs={{0,1},{1,0},{2,3},{3,2},{4,5},{5,4},{6,7},{7,6},{8,9},{9,8},{10,11... | collective-permute-start | bytes 7741448 | tf_op jit(solution)/shard_map/ppermute | solution.py:71
  361.2 7.3 %collective-permute-start.25 = (bf16[1120,768]{1,0:T(8,128)(2,1)S(1)}, bf16[1120,768]{1,0:T(8,128)(2,1)S(1)}, u32[]{:S(2)}, u32[]{:S(2)}) collective-permute-start(bf16[1120,768]{1,0:T(8,128)(2,1)S(1)} %pad_maximum_fusion.7), channel_id=1, source_target_pairs={{0,1},{1,0},{2,3},{3,2},{4,5},{5,4},{6,7},{7,6},{8,9},{9,8},{10,11... | collective-permute-start | bytes 5160968 | tf_op jit(solution)/shard_map/ppermute | solution.py:71
  363.3 27.9 %collective-permute-start.19 = (bf16[2,256,768]{2,1,0:T(8,128)(2,1)}, bf16[2,256,768]{2,1,0:T(8,128)(2,1)S(1)}, u32[]{:S(2)}, u32[]{:S(2)}) collective-permute-start(bf16[2,256,768]{2,1,0:T(8,128)(2,1)} %get-tuple-element.58), channel_id=1, source_target_pairs={{0,1},{1,0},{2,3},{3,2},{4,5},{5,4},{6,7},{7,6},{8,9},{9,8},{10,11... | collective-permute-start | bytes 2359304 | tf_op jit(solution)/shard_map/ppermute | solution.py:71
  368.9 6.2 %collective-permute-start.26 = (bf16[160,768]{1,0:T(8,128)(2,1)S(1)}, bf16[160,768]{1,0:T(8,128)(2,1)S(1)}, u32[]{:S(2)}, u32[]{:S(2)}) collective-permute-start(bf16[160,768]{1,0:T(8,128)(2,1)S(1)} %fusion.118), channel_id=1, source_target_pairs={{0,8},{1,5},{2,10},{3,7},{4,0},{5,13},{6,2},{7,15},{8,16},{9,1},{1... | collective-permute-start | bytes 737288 | tf_op jit(solution)/shard_map/ppermute | solution.py:74
  372.5 6.8 %collective-permute-start.40 = (bf16[192,768]{1,0:T(8,128)(2,1)S(1)}, bf16[192,768]{1,0:T(8,128)(2,1)S(1)}, u32[]{:S(2)}, u32[]{:S(2)}) collective-permute-start(bf16[192,768]{1,0:T(8,128)(2,1)S(1)} %fusion.113), channel_id=1, source_target_pairs={{0,8},{1,5},{2,10},{3,7},{4,0},{5,13},{6,2},{7,15},{8,16},{9,1},{1... | collective-permute-start | bytes 884744 | tf_op jit(solution)/shard_map/ppermute | solution.py:74
  374.3 16.9 %collective-permute-start.23 = (bf16[2,256,768]{2,1,0:T(8,128)(2,1)S(1)}, bf16[2,256,768]{2,1,0:T(8,128)(2,1)S(1)}, u32[]{:S(2)}, u32[]{:S(2)}) collective-permute-start(bf16[2,256,768]{2,1,0:T(8,128)(2,1)S(1)} %get-tuple-element.51), channel_id=1, source_target_pairs={{0,1},{1,0},{2,3},{3,2},{4,5},{5,4},{6,7},{7,6},{8,9},{9,8},{10,11... | collective-permute-start | bytes 2359304 | tf_op jit(solution)/shard_map/ppermute | solution.py:71
  375.4 9.8 %collective-permute-start.27 = (bf16[320,768]{1,0:T(8,128)(2,1)S(1)}, bf16[320,768]{1,0:T(8,128)(2,1)S(1)}, u32[]{:S(2)}, u32[]{:S(2)}) collective-permute-start(bf16[320,768]{1,0:T(8,128)(2,1)S(1)} %fusion.98), channel_id=1, source_target_pairs={{0,8},{1,5},{2,10},{3,7},{4,0},{5,13},{6,2},{7,15},{8,16},{9,1},{1... | collective-permute-start | bytes 1474568 | tf_op jit(solution)/shard_map/ppermute | solution.py:74
  381.7 7.6 %collective-permute-start.33 = (bf16[48,3840]{1,0:T(8,128)(2,1)S(1)}, bf16[48,3840]{1,0:T(8,128)(2,1)S(1)}, u32[]{:S(2)}, u32[]{:S(2)}) collective-permute-start(bf16[48,3840]{1,0:T(8,128)(2,1)S(1)} %fusion.108), channel_id=1, source_target_pairs={{0,8},{1,5},{2,10},{3,7},{4,0},{5,13},{6,2},{7,15},{8,16},{9,1},{1... | collective-permute-start | bytes 1105928 | tf_op jit(solution)/shard_map/ppermute | solution.py:74
  383.6 12.0 %collective-permute-start.41 = (bf16[384,768]{1,0:T(8,128)(2,1)S(1)}, bf16[384,768]{1,0:T(8,128)(2,1)S(1)}, u32[]{:S(2)}, u32[]{:S(2)}) collective-permute-start(bf16[384,768]{1,0:T(8,128)(2,1)S(1)} %fusion.86), channel_id=1, source_target_pairs={{0,8},{1,5},{2,10},{3,7},{4,0},{5,13},{6,2},{7,15},{8,16},{9,1},{1... | collective-permute-start | bytes 1769480 | tf_op jit(solution)/shard_map/ppermute | solution.py:74
  385.3 15.5 %collective-permute-start.28 = (bf16[320,768]{1,0:T(8,128)(2,1)S(1)}, bf16[320,768]{1,0:T(8,128)(2,1)S(1)}, u32[]{:S(2)}, u32[]{:S(2)}) collective-permute-start(bf16[320,768]{1,0:T(8,128)(2,1)S(1)} %fusion.100), channel_id=1, source_target_pairs={{0,8},{1,5},{2,10},{3,7},{4,0},{5,13},{6,2},{7,15},{8,16},{9,1},{1... | collective-permute-start | bytes 1474568 | tf_op jit(solution)/shard_map/ppermute | solution.py:74
  389.6 19.2 %collective-permute-start.34 = (bf16[96,3840]{1,0:T(8,128)(2,1)S(1)}, bf16[96,3840]{1,0:T(8,128)(2,1)S(1)}, u32[]{:S(2)}, u32[]{:S(2)}) collective-permute-start(bf16[96,3840]{1,0:T(8,128)(2,1)S(1)} %fusion.61), channel_id=1, source_target_pairs={{0,8},{1,5},{2,10},{3,7},{4,0},{5,13},{6,2},{7,15},{8,16},{9,1},{1... | collective-permute-start | bytes 2211848 | tf_op jit(solution)/shard_map/ppermute | solution.py:74
  395.8 24.7 %collective-permute-start.42 = (bf16[384,768]{1,0:T(8,128)(2,1)S(1)}, bf16[384,768]{1,0:T(8,128)(2,1)S(1)}, u32[]{:S(2)}, u32[]{:S(2)}) collective-permute-start(bf16[384,768]{1,0:T(8,128)(2,1)S(1)} %fusion.88), channel_id=1, source_target_pairs={{0,8},{1,5},{2,10},{3,7},{4,0},{5,13},{6,2},{7,15},{8,16},{9,1},{1... | collective-permute-start | bytes 1769480 | tf_op jit(solution)/shard_map/ppermute | solution.py:74
  401.0 19.3 %collective-permute-start.29 = (bf16[320,768]{1,0:T(8,128)(2,1)S(1)}, bf16[320,768]{1,0:T(8,128)(2,1)S(1)}, u32[]{:S(2)}, u32[]{:S(2)}) collective-permute-start(bf16[320,768]{1,0:T(8,128)(2,1)S(1)} %fusion.102), channel_id=1, source_target_pairs={{0,8},{1,5},{2,10},{3,7},{4,0},{5,13},{6,2},{7,15},{8,16},{9,1},{1... | collective-permute-start | bytes 1474568 | tf_op jit(solution)/shard_map/ppermute | solution.py:74
  409.0 19.3 %collective-permute-start.35 = (bf16[96,3840]{1,0:T(8,128)(2,1)S(1)}, bf16[96,3840]{1,0:T(8,128)(2,1)S(1)}, u32[]{:S(2)}, u32[]{:S(2)}) collective-permute-start(bf16[96,3840]{1,0:T(8,128)(2,1)S(1)} %fusion.63), channel_id=1, source_target_pairs={{0,8},{1,5},{2,10},{3,7},{4,0},{5,13},{6,2},{7,15},{8,16},{9,1},{1... | collective-permute-start | bytes 2211848 | tf_op jit(solution)/shard_map/ppermute | solution.py:74
  410.7 32.0 %collective-permute-start.20 = (bf16[4,128,768]{2,1,0:T(8,128)(2,1)S(1)}, bf16[4,128,768]{2,1,0:T(8,128)(2,1)S(1)}, u32[]{:S(2)}, u32[]{:S(2)}) collective-permute-start(bf16[4,128,768]{2,1,0:T(8,128)(2,1)S(1)} %get-tuple-element.56), channel_id=1, source_target_pairs={{0,2},{1,3},{2,0},{3,1},{4,6},{5,7},{6,4},{7,5},{8,10},{9,11},{10,... | collective-permute-start | bytes 2359304 | tf_op jit(solution)/shard_map/ppermute | solution.py:71
  420.5 10.6 %collective-permute-start.30 = (bf16[320,768]{1,0:T(8,128)(2,1)S(1)}, bf16[320,768]{1,0:T(8,128)(2,1)S(1)}, u32[]{:S(2)}, u32[]{:S(2)}) collective-permute-start(bf16[320,768]{1,0:T(8,128)(2,1)S(1)} %fusion.103), channel_id=1, source_target_pairs={{0,1},{1,0},{2,3},{3,2},{4,5},{5,4},{6,7},{7,6},{8,9},{9,8},{10,11... | collective-permute-start | bytes 1474568 | tf_op jit(solution)/shard_map/ppermute | solution.py:71
  420.8 13.7 %collective-permute-start.43 = (bf16[384,768]{1,0:T(8,128)(2,1)S(1)}, bf16[384,768]{1,0:T(8,128)(2,1)S(1)}, u32[]{:S(2)}, u32[]{:S(2)}) collective-permute-start(bf16[384,768]{1,0:T(8,128)(2,1)S(1)} %fusion.90), channel_id=1, source_target_pairs={{0,8},{1,5},{2,10},{3,7},{4,0},{5,13},{6,2},{7,15},{8,16},{9,1},{1... | collective-permute-start | bytes 1769480 | tf_op jit(solution)/shard_map/ppermute | solution.py:74
  428.5 14.0 %collective-permute-start.36 = (bf16[96,3840]{1,0:T(8,128)(2,1)S(1)}, bf16[96,3840]{1,0:T(8,128)(2,1)S(1)}, u32[]{:S(2)}, u32[]{:S(2)}) collective-permute-start(bf16[96,3840]{1,0:T(8,128)(2,1)S(1)} %fusion.65), channel_id=1, source_target_pairs={{0,8},{1,5},{2,10},{3,7},{4,0},{5,13},{6,2},{7,15},{8,16},{9,1},{1... | collective-permute-start | bytes 2211848 | tf_op jit(solution)/shard_map/ppermute | solution.py:74
  430.5 20.5 %collective-permute-start.24 = (bf16[4,128,768]{2,1,0:T(8,128)(2,1)S(1)}, bf16[4,128,768]{2,1,0:T(8,128)(2,1)S(1)}, u32[]{:S(2)}, u32[]{:S(2)}) collective-permute-start(bf16[4,128,768]{2,1,0:T(8,128)(2,1)S(1)} %get-tuple-element.49), channel_id=1, source_target_pairs={{0,2},{1,3},{2,0},{3,1},{4,6},{5,7},{6,4},{7,5},{8,10},{9,11},{10,... | collective-permute-start | bytes 2359304 | tf_op jit(solution)/shard_map/ppermute | solution.py:71
  431.2 27.2 %collective-permute-start.31 = (bf16[320,768]{1,0:T(8,128)(2,1)S(1)}, bf16[320,768]{1,0:T(8,128)(2,1)S(1)}, u32[]{:S(2)}, u32[]{:S(2)}) collective-permute-start(bf16[320,768]{1,0:T(8,128)(2,1)S(1)} %add_convert_fusion.6), channel_id=1, source_target_pairs={{0,2},{1,3},{2,0},{3,1},{4,6},{5,7},{6,4},{7,5},{8,10},{9,11},{10,... | collective-permute-start | bytes 1474568 | tf_op jit(solution)/shard_map/ppermute | solution.py:71
  434.7 24.4 %collective-permute-start.44 = (bf16[384,768]{1,0:T(8,128)(2,1)S(1)}, bf16[384,768]{1,0:T(8,128)(2,1)}, u32[]{:S(2)}, u32[]{:S(2)}) collective-permute-start(bf16[384,768]{1,0:T(8,128)(2,1)S(1)} %fusion.91), channel_id=1, source_target_pairs={{0,1},{1,0},{2,3},{3,2},{4,5},{5,4},{6,7},{7,6},{8,9},{9,8},{10,11... | collective-permute-start | bytes 1769480 | tf_op jit(solution)/shard_map/ppermute | solution.py:71
  442.6 18.2 %collective-permute-start.37 = (bf16[96,3840]{1,0:T(8,128)(2,1)S(1)}, bf16[96,3840]{1,0:T(8,128)(2,1)S(1)}, u32[]{:S(2)}, u32[]{:S(2)}) collective-permute-start(bf16[96,3840]{1,0:T(8,128)(2,1)S(1)} %fusion.66), channel_id=1, source_target_pairs={{0,1},{1,0},{2,3},{3,2},{4,5},{5,4},{6,7},{7,6},{8,9},{9,8},{10,11... | collective-permute-start | bytes 2211848 | tf_op jit(solution)/shard_map/ppermute | solution.py:71
  460.3 16.3 %collective-permute-start.45 = (bf16[384,768]{1,0:T(8,128)(2,1)S(1)}, bf16[384,768]{1,0:T(8,128)(2,1)S(1)}, u32[]{:S(2)}, u32[]{:S(2)}) collective-permute-start(bf16[384,768]{1,0:T(8,128)(2,1)S(1)} %add_convert_fusion.5), channel_id=1, source_target_pairs={{0,2},{1,3},{2,0},{3,1},{4,6},{5,7},{6,4},{7,5},{8,10},{9,11},{10,... | collective-permute-start | bytes 1769480 | tf_op jit(solution)/shard_map/ppermute | solution.py:71
  461.1 27.2 %collective-permute-start.38 = (bf16[96,3840]{1,0:T(8,128)(2,1)S(1)}, bf16[96,3840]{1,0:T(8,128)(2,1)S(1)}, u32[]{:S(2)}, u32[]{:S(2)}) collective-permute-start(bf16[96,3840]{1,0:T(8,128)(2,1)S(1)} %add_convert_fusion.4), channel_id=1, source_target_pairs={{0,2},{1,3},{2,0},{3,1},{4,6},{5,7},{6,4},{7,5},{8,10},{9,11},{10,... | collective-permute-start | bytes 2211848 | tf_op jit(solution)/shard_map/ppermute | solution.py:71
  (57 other events, 341.8 us)

commit v2 on v1

v2 whole, which is shorter than its diff:
```python
import functools

import jax
import jax.numpy as jnp
from jax import lax
from jax.experimental import pallas as pl
from jax.experimental.pallas import tpu as pltpu
from jax.sharding import PartitionSpec as P

H = 12
DH = 64
VECTOR_ROWS = 32
SUM_ROWS = 32
TILE = 256
QUERIES = 256

EPS = 1e-12
NEG = -1e30
ROOT_HALF = 0.7071067811865476
DENSITY = 0.3989422804014327
BF = jnp.bfloat16
F32 = jnp.float32
MIB = 1 << 20

QB, VB, OB, G1, S1, DB, G2, S2, UB = range(9)


def dot(a, b, left, right):
    return lax.dot_general(a, b, (((left,), (right,)), ((), ())), preferred_element_type=F32)


def normalize(rows):
    center = rows - jnp.mean(rows, axis=-1, keepdims=True)
    inverse = lax.rsqrt(jnp.mean(center * center, axis=-1, keepdims=True) + EPS)
    return center * inverse, inverse


def normalize_back(grad, normed, inverse):
    return inverse * (
        grad
        - jnp.mean(grad, axis=-1, keepdims=True)
        - normed * jnp.mean(grad * normed, axis=-1, keepdims=True)
    )


def total(a):
    return jnp.sum(a, axis=0, keepdims=True)


def params(limit=56):
    return pltpu.CompilerParams(vmem_limit_bytes=limit * MIB)


def cost(flops, moved, extra=0):
    return pl.CostEstimate(flops=int(flops), bytes_accessed=int(moved), transcendentals=int(extra))


def flat(ref, columns=slice(None)):
    a = ref[:, :, columns]
    return a.reshape(a.shape[0] * a.shape[1], a.shape[2])


def held(shape):
    return pl.BlockSpec(shape, lambda *_: (0,) * len(shape), pipeline_mode=pl.Buffered(1))


HELD = pl.BlockSpec(memory_space=pl.ANY)
SCALARS = pl.BlockSpec(memory_space=pltpu.SMEM)


def tiled(width, tile=TILE):
    return pl.BlockSpec((tile, width), lambda i: (i, 0))


def fixed(shape):
    return pl.BlockSpec(shape, lambda *_: (0,) * len(shape))


class Links:
    def __init__(self):
        self.nd = lax.axis_size("dp")
        self.nb = lax.axis_size("blk")
        self.bits = self.nb.bit_length() - 1
        self.blk = lax.axis_index("blk")
        self.dp = lax.axis_index("dp")
        n = self.nd
        self.order = list(range(0, n, 2)) + list(range(n - 1, 0, -2))
        place = {d: i for i, d in enumerate(self.order)}
        self.core = self.blk & 1
        self.sign = 1 - 2 * self.core
        self.place = jnp.where(self.dp % 2 == 0, self.dp // 2, n - 1 - self.dp // 2)
        pairs = []
        for d in range(n):
            for b in range(self.nb):
                step = 1 if b % 2 == 0 else -1
                target = self.order[(place[d] + step) % n]
                pairs.append((d * self.nb + b, target * self.nb + b))
        self.pairs = pairs
        far = n // 2
        at = [self.dp]
        at += [self.shard_at(-self.sign * s) for s in range(1, far)]
        at += [self.shard_at(self.sign * s) for s in range(1, far)]
        at += [self.shard_at(far), self.core]
        self.sources = jnp.stack(at).astype(jnp.int32)
        at = [self.shard_at(-self.sign * s) for s in range(1, far)]
        at += [self.shard_at(far)]
        at += [self.shard_at(self.sign * s) for s in range(1, far)]
        at += [self.dp]
        self.targets = jnp.stack(at).astype(jnp.int32)

    def swap(self, a, bit):
        return lax.ppermute(a, "blk", [(i, i ^ (1 << bit)) for i in range(self.nb)])

    def step(self, a):
        return lax.ppermute(a, ("dp", "blk"), self.pairs)

    def shard_at(self, offset):
        n = self.nd
        at = (self.place + offset) % n
        return jnp.where(at < n // 2, 2 * at, 2 * (n - 1 - at) + 1)

    def to_rows(self, a):
        for bit in reversed(range(self.bits)):
            half = a.shape[0] // 2
            mine = (self.blk >> bit) & 1
            keep = lax.dynamic_slice_in_dim(a, mine * half, half, 0)
            send = lax.dynamic_slice_in_dim(a, (1 - mine) * half, half, 0)
            got = self.swap(send, bit)
            yield got
            a = jnp.concatenate([keep, got], axis=1)
        yield a

    def from_rows(self, a):
        for bit in range(self.bits):
            half = a.shape[1] // 2
            mine = (self.blk >> bit) & 1
            keep, got = a[:, :half], self.swap(a[:, half:], bit)
            yield got
            a = jnp.where(
                mine == 0,
                jnp.concatenate([keep, got], 0),
                jnp.concatenate([got, keep], 0),
            )
        yield a

    def gather(self, piece, waits=()):
        n, m = self.nd, piece.shape[0]
        mine, other, now = [], [], piece
        waits = dict(enumerate(waits))
        for i in range(n // 2 - 1):
            if i in waits:
                now = after(now, waits[i])
            now = self.step(now)
            mine.append(now)
            other.append(self.swap(now, 0))
        far = self.step(lax.dynamic_slice_in_dim(now, self.core * (m // 2), m // 2, 0))
        return [piece] + mine + other + [far, self.swap(far, 0)]

    def whole(self, pieces):
        n = self.nd
        out = jnp.zeros((n,) + pieces[0].shape, pieces[0].dtype)
        for i, a in enumerate(pieces[:-2]):
            out = lax.dynamic_update_slice(out, a[None], (self.sources[i], 0, 0))
        a, b = pieces[-2:]
        far = jnp.where(self.core == 0, jnp.concatenate([a, b], 0), jnp.concatenate([b, a], 0))
        return lax.dynamic_update_slice(out, far[None], (self.sources[n - 1], 0, 0))

    def split(self, parts):
        pick = lambda i: lax.dynamic_index_in_dim(parts, self.targets[i], 0, keepdims=False)
        half = self.nd // 2
        return (
            jnp.stack([pick(i) for i in range(half)]),
            jnp.stack([pick(i) for i in range(half - 1, self.nd)]),
        )

    def scatter(self, send, keep):
        n, m = self.nd, keep.shape[1]
        far = n // 2
        got = self.swap(send, 0)
        yield got
        halved = lambda a: lax.dynamic_slice_in_dim(a, self.core * (m // 2), m // 2, 0).astype(F32)
        acc = halved(keep[0]) + halved(got[far - 1])
        moved = self.step(acc.astype(BF))
        yield moved
        zero = jnp.zeros((m // 2,) + moved.shape[1:], BF)
        moved = jnp.where(
            self.core == 0,
            jnp.concatenate([moved, zero], 0),
            jnp.concatenate([zero, moved], 0),
        )
        for s in range(far - 1, 0, -1):
            acc = keep[s].astype(F32) + got[s - 1].astype(F32) + moved.astype(F32)
            moved = self.step(acc.astype(BF))
            yield moved
        acc = keep[far].astype(F32) + moved.astype(F32)
        for bit in range(self.bits):
            low = acc.astype(BF)
            moved = self.swap(low, bit)
            yield moved
            acc = low.astype(F32) + moved.astype(F32)
        yield acc


class Group:
    def __init__(self, arrays, parts, pieces, width):
        self.arrays, self.parts, self.pieces, self.width = arrays, parts, pieces, width
        self.n_refs = len(arrays)
        self.specs = [held(a.shape) for a in arrays]

    def scratch(self, names, n):
        shape = lambda rows: (n, rows) if self.pieces else (1, n * rows)
        return [
            pltpu.VMEM(shape(rows) + (self.width,), BF) for rows, name in self.parts if name in names
        ]

    def fetch(self, refs, sources, names, into):
        into = dict(zip(names, into))
        if not self.pieces:
            for (_, name), ref in zip(self.parts, refs):
                if name in names:
                    into[name][0] = ref[...]
            return
        n = self.n_refs - 1
        half = sum(rows for rows, _ in self.parts) // 2
        starts = [sum(rows for rows, _ in self.parts[:i]) for i in range(len(self.parts))]
        for i in range(n - 1):
            for start, (rows, name) in zip(starts, self.parts):
                if name in names:
                    into[name][sources[i]] = refs[i][start : start + rows]
        for core in range(2):

            @pl.when(sources[n] == core)
            def _(core=core):
                for start, (rows, name) in zip(starts, self.parts):
                    for h in range(2):
                        low, high = max(start, h * half), min(start + rows, (h + 1) * half)
                        if name in names and low < high:
                            ref = refs[n - 1] if h == core else refs[n]
                            into[name][sources[n - 1], low - start : high - start] = ref[
                                low - h * half : high - h * half
                            ]


def pack(weights, vectors):
    shard, dim = weights[0].shape

    def kernel(*refs):
        mats, vecs, out_ref, table = refs[: len(weights)], refs[len(weights) : -2], refs[-2], refs[-1]
        for i, ref in enumerate(mats):
            out_ref[i * shard : (i + 1) * shard] = ref[...]
        table[...] = jnp.zeros_like(table)
        line = 0
        for ref in vecs:
            a = ref[...].astype(F32)
            for t in range(a.shape[0] // shard):
                table[line : line + 1, :shard] = a[t * shard : (t + 1) * shard].reshape(1, shard)
                line += 1
        blank = jnp.zeros((VECTOR_ROWS, dim - 128), F32)
        out_ref[len(mats) * shard :] = jnp.concatenate([table[...], blank], 1).astype(BF)

    return pl.pallas_call(
        kernel,
        out_shape=jax.ShapeDtypeStruct((len(weights) * shard + VECTOR_ROWS, dim), BF),
        scratch_shapes=[pltpu.VMEM((VECTOR_ROWS, 128), F32)],
        compiler_params=params(),
        cost_estimate=cost(0, 4 * len(weights) * shard * dim),
        name="pack",
    )(*weights, *vectors)


def after(a, *others):
    return lax.optimization_barrier((a,) + others)[0]


def lay(links, group, names, spread=None):
    n = links.nd
    k = group.n_refs
    sizes = {name: rows for rows, name in group.parts}
    tables = 0 if spread is None else 1

    def kernel(*refs):
        sources, pieces = refs[0], refs[1 : 1 + k]
        outs = refs[1 + k + tables :]
        group.fetch(pieces, sources, names, outs)
        if tables:
            lines = outs[-2][...].astype(F32).reshape(n, VECTOR_ROWS, group.width)[:, :, :128]
            wide = jnp.concatenate([lines[j] for j in range(n)], 1).astype(BF)
            outs[-1][...] = dot(wide, refs[1 + k][...], 1, 0)

    shapes = [((n, sizes[x]) if group.pieces else (1, n * sizes[x])) + (group.width,) for x in names]
    out_shape = [jax.ShapeDtypeStruct(x, BF) for x in shapes]
    args = [links.sources, *group.arrays]
    specs = [SCALARS] + group.specs
    if tables:
        args.append(spread)
        specs.append(held(spread.shape))
        out_shape.append(jax.ShapeDtypeStruct((VECTOR_ROWS, group.width), F32))
    out = pl.pallas_call(
        kernel,
        grid=(1,),
        in_specs=specs,
        out_specs=[held(x.shape) for x in out_shape],
        out_shape=out_shape,
        compiler_params=params(),
        cost_estimate=cost(0, sum(4 * x.size for x in out_shape)),
        name="lay",
    )(*args)
    return [x.reshape(-1, group.width) for x in out]


def head_masks(width):
    lane = lax.broadcasted_iota(jnp.int32, (1, width), 1)
    return [lane // DH == h for h in range(width // DH)]


def fill_bias(bias, down_ref, across_ref):
    bias[...] = jnp.where(down_ref[...][:, :1] == across_ref[0], 0.0, NEG)


def attend(q, k, v, down, across):
    rows, _, length = across.shape
    dim = q.shape[1]
    pairs = dim // 128

    def kernel(down_ref, across_ref, q_ref, k_ref, v_ref, o_ref, log_ref, bias):
        @pl.when(pl.program_id(1) == 0)
        def _():
            fill_bias(bias, down_ref, across_ref)

        masks = head_masks(128)
        keys, values_t = k_ref[...], v_ref[...].astype(F32).T.astype(BF)
        scaled = q_ref[...].astype(F32) * DH**-0.5
        for at in range(0, length, QUERIES):
            span = slice(at, at + QUERIES)
            outs = []
            for h, mask in enumerate(masks):
                one = jnp.where(mask, scaled[span], 0.0).astype(BF)
                s = dot(keys, one, 1, 1) + bias[:, span]
                top = jnp.max(s, axis=0, keepdims=True)
                e = jnp.exp(s - top)
                sums = jnp.sum(e, axis=0, keepdims=True)
                o = dot(values_t[h * DH : (h + 1) * DH], e.astype(BF), 1, 0)
                outs.append(o / sums)
                log_ref[0, 0, h : h + 1, span] = top + jnp.log(sums)
            o_ref[span] = jnp.concatenate(outs, 0).T.astype(BF)

    block = pl.BlockSpec((length, 128), lambda r, h: (r, h))
    return pl.pallas_call(
        kernel,
        grid=(rows, pairs),
        in_specs=[
            pl.BlockSpec((length, 128), lambda r, h: (r, 0)),
            pl.BlockSpec((1, 1, length), lambda r, h: (r, 0, 0)),
            block,
            block,
            block,
        ],
        out_specs=[block, pl.BlockSpec((1, 1, 2, length), lambda r, h: (r, h, 0, 0))],
        out_shape=[
            jax.ShapeDtypeStruct(q.shape, BF),
            jax.ShapeDtypeStruct((rows, pairs, 2, length), F32),
        ],
        scratch_shapes=[pltpu.VMEM((length, length), F32)],
        compiler_params=params(),
        cost_estimate=cost(
            16 * rows * H * length * length * DH, 8 * rows * length * dim, rows * H * length * length
        ),
        name="attend",
    )(down, across, q, k, v)


def attend_back(q, k, v, g, logs, down, across, row, grads):
    rows, _, length = across.shape
    dim = q.shape[1]
    pairs = dim // 128

    grads = grads or ()

    def kernel(down_ref, across_ref, q_ref, k_ref, v_ref, g_ref, log_ref, *refs):
        gq_ref, gk_ref, gv_ref, bias = refs[len(grads) :]

        @pl.when(pl.program_id(0) == 0)
        def _():
            fill_bias(bias, down_ref, across_ref)

        masks = head_masks(128)
        keys, values, keys_t = k_ref[...], v_ref[...], k_ref[...].astype(F32).T.astype(BF)
        scaled = q_ref[...].astype(F32) * DH**-0.5
        grad = g_ref[...].astype(F32)
        scaled_low = scaled.astype(BF)
        gk = [0.0] * len(masks)
        gv = [0.0] * len(masks)
        for at in range(0, length, QUERIES):
            span = slice(at, at + QUERIES)
            outs = []
            for h, mask in enumerate(masks):
                one = jnp.where(mask, scaled[span], 0.0).astype(BF)
                s = dot(keys, one, 1, 1) + bias[:, span]
                p = jnp.exp(s - log_ref[0, 0, h : h + 1, span])
                one_g = jnp.where(mask, grad[span], 0.0).astype(BF)
                t = p * dot(values, one_g, 1, 1)
                gs = (t - p * jnp.sum(t, axis=0, keepdims=True)).astype(BF)
                gv[h] += dot(p.astype(BF), g_ref[span], 1, 0)
                gk[h] += dot(gs, scaled_low[span], 1, 0)
                outs.append(dot(keys_t[h * DH : (h + 1) * DH], gs, 1, 0))
            gq_ref[span] = (jnp.concatenate(outs, 0).T * DH**-0.5).astype(BF)
        gk_ref[...] = jnp.where(masks[0], gk[0], gk[1]).astype(BF)
        gv_ref[...] = jnp.where(masks[0], gv[0], gv[1]).astype(BF)

    block = pl.BlockSpec((length, 128), lambda h: (row, h))
    out = jax.ShapeDtypeStruct(q.shape, BF)
    return pl.pallas_call(
        kernel,
        grid=(pairs,),
        in_specs=[
            pl.BlockSpec((length, 128), lambda h: (row, 0)),
            pl.BlockSpec((1, 1, length), lambda h: (row, 0, 0)),
            block,
            block,
            block,
            block,
            pl.BlockSpec((1, 1, 2, length), lambda h: (row, h, 0, 0)),
        ]
        + [HELD] * len(grads),
        out_specs=[block] * 3,
        out_shape=[out] * 3,
        input_output_aliases={7 + i: i for i in range(len(grads))},
        scratch_shapes=[pltpu.VMEM((length, length), F32)],
        compiler_params=params(),
        cost_estimate=cost(
            40 * H * length * length * DH, 14 * length * dim, H * length * length
        ),
        name="attend_back",
    )(down, across, q, k, v, g, logs, *grads)


def halves(n, rows, width):
    return [
        jax.ShapeDtypeStruct((n // 2, rows, width), BF),
        jax.ShapeDtypeStruct((n // 2 + 1, rows, width), BF),
    ]


def outer_rows(links, a, b):
    tokens, wide = a.shape
    dim = b.shape[1]
    n = links.nd
    rows = wide // n
    far = n // 2

    def kernel(targets, a_ref, b_ref, send_ref, keep_ref):
        i = pl.program_id(0)
        low = dot(a_ref[...], b_ref[...], 0, 0).astype(BF)

        @pl.when(i < far)
        def _():
            send_ref[0] = low

        @pl.when(i >= far - 1)
        def _():
            keep_ref[0] = low

    return pl.pallas_call(
        kernel,
        grid_spec=pltpu.PrefetchScalarGridSpec(
            num_scalar_prefetch=1,
            grid=(n,),
            in_specs=[
                pl.BlockSpec((tokens, rows), lambda i, at: (0, at[i])),
                pl.BlockSpec((tokens, dim), lambda i, at: (0, 0)),
            ],
            out_specs=[
                pl.BlockSpec((1, rows, dim), lambda i, at: (jnp.minimum(i, far - 1), 0, 0)),
                pl.BlockSpec((1, rows, dim), lambda i, at: (jnp.maximum(i - far + 1, 0), 0, 0)),
            ],
        ),
        out_shape=halves(n, rows, dim),
        compiler_params=params(),
        cost_estimate=cost(2 * tokens * dim * wide, 2 * (tokens + dim) * wide),
        name="outer_rows",
    )(links.targets, a, b)


def store_shards(targets, rows, block, value, send_ref, keep_ref, start):
    n = targets.shape[0]
    far = n // 2
    block[...] = value.astype(BF).reshape(block.shape)
    for i in range(n):
        piece = block[targets[i]]
        if i < far:
            send_ref[i, pl.ds(start, rows), :] = piece
        if i >= far - 1:
            keep_ref[i - far + 1, pl.ds(start, rows), :] = piece


def outer_columns(links, pairs):
    tokens, dim = pairs[0][0].shape
    n = links.nd
    rows = dim // n
    far = n // 2
    (a0, b0), (a1, b1) = pairs
    steps = b1.shape[1] // dim + 1

    def kernel(targets, a0_ref, b0_ref, a1_ref, b1_ref, send_ref, keep_ref, block):
        i = pl.program_id(0)

        @pl.when(i == 0)
        def _():
            value = dot(a0_ref[...], b0_ref[...], 0, 0)
            store_shards(targets, rows, block, value, send_ref, keep_ref, 0)

        @pl.when(i > 0)
        def _():
            value = dot(a1_ref[...], b1_ref[...], 0, 0)
            store_shards(targets, rows, block, value, send_ref, keep_ref, 0)

    whole = pl.BlockSpec((tokens, dim), lambda i: (0, 0))
    width = dim * steps
    return pl.pallas_call(
        kernel,
        grid=(steps,),
        in_specs=[
            SCALARS,
            whole,
            whole,
            whole,
            pl.BlockSpec((tokens, dim), lambda i: (0, jnp.maximum(i - 1, 0))),
        ],
        out_specs=[
            pl.BlockSpec((far, rows, dim), lambda i: (0, 0, i)),
            pl.BlockSpec((far + 1, rows, dim), lambda i: (0, 0, i)),
        ],
        out_shape=halves(n, rows, width),
        scratch_shapes=[pltpu.VMEM((n, rows, dim), BF)],
        compiler_params=params(),
        cost_estimate=cost(2 * tokens * dim * width, 2 * (tokens + dim) * width),
        name="outer_columns",
    )(links.targets, a0, b0, a1, b1)


def outer_last(links, x, grads, sums, spread):
    tokens, dim = x.shape
    n = links.nd
    rows = dim // n
    far = n // 2
    deep = len(grads) * rows + SUM_ROWS

    def kernel(targets, x_ref, q_ref, k_ref, v_ref, sums_ref, spread_ref, send_ref, keep_ref, block):
        for t, ref in enumerate((q_ref, k_ref, v_ref)):
            store_shards(
                targets, rows, block, dot(x_ref[...], ref[...], 0, 0), send_ref, keep_ref, t * rows
            )
        line = lax.broadcasted_iota(jnp.int32, (SUM_ROWS, 1), 0)
        table = sums_ref[...]
        table = jnp.where(line == QB, total(q_ref[...].astype(F32)), table)
        table = jnp.where(line == VB, total(v_ref[...].astype(F32)), table)
        table = table.astype(BF)
        blank = jnp.zeros((SUM_ROWS, dim - 128), F32)
        start = len(grads) * rows
        for i in range(n):
            part = dot(table, spread_ref[targets[i]], 1, 1)
            part = jnp.concatenate([part, blank], 1).astype(BF)
            if i < far:
                send_ref[i, pl.ds(start, SUM_ROWS), :] = part
            if i >= far - 1:
                keep_ref[i - far + 1, pl.ds(start, SUM_ROWS), :] = part

    whole = fixed((tokens, dim))
    return pl.pallas_call(
        kernel,
        grid=(1,),
        in_specs=[SCALARS] + [whole] * 4 + [fixed(sums.shape), fixed((n, 128, dim))],
        out_specs=[fixed((far, deep, dim)), fixed((far + 1, deep, dim))],
        out_shape=halves(n, deep, dim),
        scratch_shapes=[pltpu.VMEM((n, rows, dim), BF)],
        compiler_params=params(),
        cost_estimate=cost(6 * tokens * dim * dim, 8 * tokens * dim + 6 * dim * dim),
        name="outer_last",
    )(links.targets, x, *grads, sums, spread.reshape(n, 128, dim))


def local(
    tokens,
    fragments,
    cotangent,
    query_weight,
    query_bias,
    key_weight,
    value_weight,
    value_bias,
    out_weight,
    out_bias,
    first_gain,
    first_shift,
    up_weight,
    up_bias,
    down_weight,
    down_bias,
    second_gain,
    second_shift,
):
    links = Links()
    n = links.nd
    shard, dim = query_weight.shape
    times = up_bias.shape[0] // shard
    aligned = shard % 32 == 0

    vectors = [query_bias, value_bias, out_bias, first_gain, first_shift, down_bias, second_gain, second_shift]
    vectors.append(up_bias)
    piece = pack([query_weight, key_weight, value_weight, out_weight], vectors)
    ids_steps = links.to_rows(fragments)
    ids_moved = next(ids_steps)
    x_steps = links.to_rows(after(tokens, ids_moved))
    x_moved = next(x_steps)
    first = links.gather(piece, [piece, ids_moved, x_moved])
    *_, ids = ids_steps
    *_, x = x_steps
    rows, length = ids.shape
    ups = links.gather(up_weight, [first[n // 2 - 1]])
    downs = links.gather(down_weight, [ups[1]])
    *_, g = links.to_rows(after(cotangent, first[-1]))

    parts = [(shard, name) for name in "qkvo"] + [(VECTOR_ROWS, "vec")]
    if not aligned:
        w = links.whole(first)
        first = [w[:, i * shard : (i + 1) * shard].reshape(dim, dim) for i in range(4)]
        first.append(w[:, 4 * shard :].reshape(n * VECTOR_ROWS, dim))
        ups = [links.whole(ups).reshape(dim, -1)]
        downs = [links.whole(downs).reshape(-1, dim)]
    first = Group(first, parts, aligned, dim)
    ups = Group(ups, [(shard, "u")], aligned, times * dim)
    downs = Group(downs, [(times * shard, "d")], aligned, dim)

    at = lax.broadcasted_iota(jnp.int32, (n * 128, dim), 0)
    lane = lax.broadcasted_iota(jnp.int32, (n * 128, dim), 1)
    spread = ((at % 128 < shard) & (lane == at // 128 * shard + at % 128)).astype(BF)

    x = x.reshape(-1, dim)
    g = g.reshape(-1, dim)
    across = ids[:, None, :]
    down = jnp.broadcast_to(ids.reshape(-1, 1), (rows * length, 128))

    q_w, k_w, v_w, o_w, _, table = lay(links, first, ["q", "k", "v", "o", "vec"], spread)
    row = lambda i: table[i : i + 1]
    up_row = table[UB : UB + times].reshape(times, n, shard).transpose(1, 0, 2).reshape(1, -1)
    q = (dot(x, q_w, 1, 0) + row(QB)).astype(BF)
    k = dot(x, k_w, 1, 0).astype(BF)
    v = (dot(x, v_w, 1, 0) + row(VB)).astype(BF)
    heads = lambda a: a.reshape(rows, length, H, DH).transpose(0, 2, 1, 3)
    merge = lambda a: a.transpose(0, 2, 1, 3).reshape(-1, dim)
    qh, kh, vh = heads(q), heads(k), heads(v)
    allowed = (ids[:, :, None] == ids[:, None, :])[:, None]
    scores = jnp.einsum("rhqd,rhkd->rhqk", qh, kh, preferred_element_type=F32) * DH**-0.5
    scores = jnp.where(allowed, scores, NEG)
    e = jnp.exp(scores - jnp.max(scores, axis=-1, keepdims=True))
    probs = e / jnp.sum(e, axis=-1, keepdims=True)
    plow = probs.astype(BF)
    attended = merge(jnp.einsum("rhqk,rhkd->rhqd", plow, vh, preferred_element_type=F32).astype(BF))
    n1, inv1 = normalize(x.astype(F32) + dot(attended, o_w, 1, 0) + row(OB))
    hidden = n1 * row(G1) + row(S1)
    low = hidden.astype(BF)
    (u_w,) = lay(links, ups, ["u"])
    before = dot(low, u_w, 1, 0) + up_row
    phi = 0.5 * (1.0 + lax.erf(before * ROOT_HALF))
    active = (before * phi).astype(BF)
    slope = (phi + before * (DENSITY * jnp.exp(-0.5 * before * before))).astype(BF)
    (d_w,) = lay(links, downs, ["d"])
    n2, inv2 = normalize(hidden + dot(active, d_w, 1, 0) + row(DB))
    result = (n2 * row(G2) + row(S2)).astype(BF)
    grad = g.astype(F32)
    g_r2 = normalize_back(grad * row(G2), n2, inv2)
    g_second = g_r2.astype(BF)
    sums2 = jnp.concatenate([total(g_second.astype(F32)), total(grad * n2), total(grad)], 0)
    if aligned and not dim:
        send, keep = outer_rows(links, active, g_second)
    else:
        send, keep = links.split(dot(active, g_second, 0, 0).astype(BF).reshape(n, -1, dim))
    down_steps = links.scatter(send, keep)
    result_steps = links.from_rows(result.reshape(rows, length, dim))
    g_before = (dot(g_second, d_w, 1, 1) * slope.astype(F32)).astype(BF)
    sums_up = total(g_before.astype(F32))
    g_before = after(g_before, next(down_steps), next(result_steps))
    g_hidden = g_r2 + dot(g_before, u_w, 1, 1)
    g_r1 = normalize_back(g_hidden * row(G1), n1, inv1)
    g_branch = g_r1.astype(BF)
    sums1 = jnp.concatenate([total(g_branch.astype(F32)), total(g_hidden * n1), total(g_hidden)], 0)
    g_att = dot(g_branch, o_w, 1, 1).astype(BF)
    g_branch = after(g_branch, next(down_steps), next(result_steps))
    if aligned and not dim:
        send, keep = outer_columns(links, [(attended, g_branch), (low, g_before)])
    else:
        both = [dot(attended, g_branch, 0, 0), dot(low, g_before, 0, 0)]
        send, keep = links.split(jnp.concatenate(both, 1).astype(BF).reshape(n, shard, -1))
    up_steps = links.scatter(send, keep)
    g_att = after(g_att, next(down_steps), keep)
    g_att = after(g_att, next(down_steps), next(up_steps))
    gh = heads(g_att)
    gv = jnp.einsum("rhqk,rhqd->rhkd", plow, gh, preferred_element_type=F32)
    gp = jnp.einsum("rhqd,rhkd->rhqk", gh, vh, preferred_element_type=F32)
    gs = (probs * (gp - jnp.sum(probs * gp, axis=-1, keepdims=True))).astype(BF)
    gq = jnp.einsum("rhqk,rhkd->rhqd", gs, kh, preferred_element_type=F32) * DH**-0.5
    gk = jnp.einsum("rhqk,rhqd->rhkd", gs, qh, preferred_element_type=F32) * DH**-0.5
    gq, gk, gv = (merge(a.astype(BF)) for a in (gq, gk, gv))
    gq = after(gq, next(down_steps), next(up_steps))
    up_sums = sums_up[0].reshape(n, times, shard).transpose(1, 0, 2).reshape(times, dim)
    zero = jnp.zeros((1, dim), F32)
    sums = jnp.concatenate([zero, zero, sums1, sums2, up_sums], 0)
    sums = jnp.pad(sums, ((0, SUM_ROWS - sums.shape[0]), (0, 0)))
    if aligned and not dim:
        send, keep = outer_last(links, x, (gq, gk, gv), sums, spread)
    else:
        sums = sums.at[QB].set(jnp.sum(gq.astype(F32), 0)).at[VB].set(jnp.sum(gv.astype(F32), 0))
        sums = jnp.pad(
            sums.astype(BF).reshape(SUM_ROWS, n, shard).transpose(1, 0, 2),
            ((0, 0), (0, 0), (0, dim - shard)),
        )
        each = [dot(x, a, 0, 0).astype(BF).reshape(n, shard, dim) for a in (gq, gk, gv)]
        send, keep = links.split(jnp.concatenate(each + [sums], 1))
    last_steps = links.scatter(send, keep)
    gq = after(gq, next(down_steps), next(up_steps), keep)
    g_x = (g_r1 + dot(gq, q_w, 1, 1) + dot(gk, k_w, 1, 1) + dot(gv, v_w, 1, 1)).astype(BF)
    g_x = after(g_x, next(down_steps), next(up_steps), next(last_steps))
    *_, g_x = links.from_rows(g_x.reshape(rows, length, dim))
    *_, result = result_steps
    *_, grad_down = down_steps
    *_, both = up_steps
    *_, last = last_steps
    grad_q, grad_k, grad_v = (last[i * shard : (i + 1) * shard] for i in range(3))
    vecs = last[3 * shard :, :shard]
    return (
        result,
        g_x,
        grad_q,
        vecs[QB],
        grad_k,
        grad_v,
        vecs[VB],
        both[:, :dim],
        vecs[OB],
        vecs[G1],
        vecs[S1],
        both[:, dim:],
        vecs[UB : UB + times].reshape(-1),
        grad_down,
        vecs[DB],
        vecs[G2],
        vecs[S2],
    )


def solution(mesh):
    three, two, one = P("dp", "blk", None), P("dp", None), P("dp")
    weights = (two, one, two, two, one, two, one, one, one, two, one, two, one, one, one)
    return jax.shard_map(
        local,
        mesh=mesh,
        in_specs=(three, P("dp", "blk"), three) + weights,
        out_specs=(three, three) + weights,
        check_vma=False,
    )
```

time: 497 us -> 485 us (0.976)
  local copies, waits for them, and re-layouts: 112 us -> 50.4 us
  waiting for transfers between devices: 101 us -> 122 us
  Pallas kernels: 0 us -> 17.5 us
  other arithmetic: 64.8 us -> 78.4 us
    dynamic_update_slice x21 -> x0, local copies, waits for them, and re-layouts: 25.2 us -> none  [gather(): lax.dynamic_update_slice(w, a[None], (at,) + (0,) * a.ndim)]
    ppermute x24, waiting for transfers between devices: 63.8 us -> 85.8 us  [step(): return lax.ppermute(a, ('dp', 'blk'), self.pairs)]
    pallas_call x0 -> x4, Pallas kernels: none -> 17.5 us  [the longest x3 15.3 us: lay(): pl.pallas_call(kernel, grid=(1,), in_specs=specs, out_specs=[held(x.shape...]
    convert_element_type x26 -> x7, local copies, waits for them, and re-layouts: 22.5 us -> 10.7 us  [the longest x3 4.86 us: local(): gq, gk, gv = (merge(a.astype(BF)) for a in (gq, gk, gv))]
    convert_element_type x21 -> x14, other arithmetic: 28.7 us -> 40.2 us  [the longest x1 21.2 us: local(): gs = (probs * (gp - jnp.sum(probs * gp, axis=-1, keepdims=True))).astype(BF)]
    concatenate x4 -> x2, local copies, waits for them, and re-layouts: 8.12 us -> 0.07 us  [local(): sums = jnp.concatenate([zero, zero, sums1, sums2, up_sums], 0)]
    concatenate x12 -> x7, other arithmetic: 15.2 us -> 7.38 us  [the longest x5 4.89 us: to_rows(): a = jnp.concatenate([keep, got], axis=1)]
    reshape x6 -> x9, local copies, waits for them, and re-layouts: 14.5 us -> 9.35 us  [the longest x4 8.38 us: local(): heads = lambda a: a.reshape(rows, length, H, DH).transpose(0, 2, 1, 3)]
  transfers between devices with their start and end apart: 46 -> 55, of which waited for: 21 -> 20; matrix products, arithmetic and copies ran while one was open for 33% -> 52% of each run, Pallas kernels for 0% -> 2%
where the time goes in v2:
time: 485 us; the launch traced here: 480 us
  matrix products  158 us (33%)
  waiting for transfers between devices  122 us (25%)
  other arithmetic  78.4 us (16%)
  starting transfers between devices  51 us (11%)
  local copies, waits for them, and re-layouts  50.4 us (10%)
  Pallas kernels  17.5 us (4%)
    dot_general x18, matrix products, dot(): lax.dot_general(a, b, (((left,), (right,)), ((), ())), preferred_element_...  86.7 us
    ppermute x24, waiting for transfers between devices, step(): return lax.ppermute(a, ('dp', 'blk'), self.pairs)  85.8 us
    ppermute x31, waiting for transfers between devices, swap(): return lax.ppermute(a, 'blk', [(i, i ^ 1 << bit) for i in range(self.nb)])  36.5 us
    ppermute x24, starting transfers between devices, step(): return lax.ppermute(a, ('dp', 'blk'), self.pairs)  36.1 us
    convert_element_type x1, other arithmetic, local(): gs = (probs * (gp - jnp.sum(probs * gp, axis=-1, keepdims=True))).astype(BF)  21.2 us
    dot_general x1, matrix products, local(): gp = jnp.einsum('rhqd,rhkd->rhqk', gh, vh, preferred_element_type=F32)  16.7 us
    convert_element_type x12, other arithmetic, scatter(): moved = self.step(acc.astype(BF))  16.5 us
    pallas_call x3, Pallas kernels, lay(): pl.pallas_call(kernel, grid=(1,), in_specs=specs, out_specs=[held(x.shape...  15.3 us
  transfers between devices with their start and end apart: 55, of which 20 were waited for; matrix products, arithmetic and copies ran while one was open for 52% of the time, Pallas kernels for 2%

profile of v2, /device:TPU:0, one launch (start us, length us, event | category | flops | bytes accessed | tf_op | source)
XLA Modules:
  0.0 479.8 jit_solution(14367876667858482089)
XLA Ops:
  2.8 3.0 collective-permute-start.4
  16.6 13.3 %collective-permute-done.1 = bf16[4,128,768]{2,1,0:T(8,128)(2,1)S(1)} collective-permute-done((bf16[4,128,768]{2,1,0:T(8,128)(2,1)S(1)}, bf16[4,128,768]{2,1,0:T(8,128)(2,1)S(1)}, u32[]{:S(2)}, u32[]{:S(2)}) %collective-permute-start.1) | collective-permute-done | bytes 786464 | tf_op jit(solution)/shard_map/ppermute | solution.py:112
  34.5 8.3 %collective-permute-done.6.refs_4_ = bf16[416,768]{1,0:T(8,128)(2,1)S(1)} collective-permute-done((bf16[416,768]{1,0:T(8,128)(2,1)}, bf16[416,768]{1,0:T(8,128)(2,1)S(1)}, u32[]{:S(2)}, u32[]{:S(2)}) %collective-permute-start.6) | collective-permute-done | bytes 639008 | tf_op jit(solution)/shard_map/ppermute | solution.py:115
  45.0 2.5 fusion.27.refs_10_
  52.4 3.8 collective-permute-done.12.refs_2_
  58.1 5.8 %lay.3 = (bf16[8,96,768]{2,1,0:T(8,128)(2,1)}, bf16[8,96,768]{2,1,0:T(8,128)(2,1)}, bf16[8,96,768]{2,1,0:T(8,128)(2,1)}, bf16[8,96,768]{2,1,0:T(8,128)(2,1)}, bf...) custom-call(s32[9]{0:T(128)} %stack.35.refs_0_, bf16[416,768]{1,0:T(8,128)(2,1)} %pack.1.refs_1_, ...), custom_call_target="tpu_custom_call" | custom-call | bytes 10321920 | tf_op jit(solution)/shard_map/lay/pallas_call | solution.py:298
  65.6 3.8 add_convert_fusion.2
  73.5 3.8 add_convert_fusion.3
  79.0 2.4 reshape.282
  87.7 14.8 %fusion.116 = (f32[2,12,512]{2,1,0:T(8,128)S(1)}, f32[2,12,512,512]{2,3,1,0:T(8,128)}) fusion(pred[2,512,512]{1,2,0:T(8,128)(4,1)} %broadcast_compare_fusion, bf16[2,12,512,64]{2,0,3,1:T(2,128)(2,1)S(1)} %bitcast.210, bf16[2,12,512,64]{2,0,3,1:T(2,128)(2,1)} %bitcast.243), kind=kOutput, calls=%fused_computation.250 | convolution fusion | flops 830472704 | bytes 28884992 | tf_op jit(solution)/shard_map/sub | solution.py:655
  102.5 9.9 %fusion.43 = bf16[2,512,12,64]{1,3,2,0:T(8,128)(2,1)S(1)} fusion(bf16[2,12,512,64]{2,0,3,1:T(2,128)(2,1)S(1)} %bitcast.245, f32[2,12,512,512]{2,3,1,0:T(8,128)} %get-tuple-element.147, f32[2,12,512]{2,1,0:T(8,128)S(1)} %get-tuple-element.146), kind=kOutput, calls=%fused_computation.115 | convolution fusion | flops 818675712 | bytes 28360704 | tf_op jit(solution)/shard_map/rhqk,rhkd->rhqd/dot_general | solution.py:658
  119.4 2.4 fusion.79
  121.8 9.2 %collective-permute-done.14.refs_4_ = bf16[96,3072]{1,0:T(8,128)(2,1)} collective-permute-done((bf16[96,3072]{1,0:T(8,128)(2,1)}, bf16[96,3072]{1,0:T(8,128)(2,1)}, u32[]{:S(2)}, u32[]{:S(2)}) %collective-permute-start.14) | collective-permute-done | bytes 589856 | tf_op jit(solution)/shard_map/ppermute | solution.py:115
  135.8 3.0 collective-permute-done.18.refs_8_
  140.9 4.3 collective-permute-done.22.refs_4_
  151.4 4.7 lay.4
  156.6 12.2 %multiply_convert_fusion.2 = (bf16[1024,3072]{1,0:T(8,128)(2,1)}, f32[1024,3072]{1,0:T(8,128)}) fusion(f32[3072]{0:T(1024)S(1)} %copy-done.46, bf16[768,3072]{1,0:T(8,128)(2,1)} %bitcast.229, f32[1024,768]{1,0:T(8,128)S(1)} %get-tuple-element.101, f32[768]{0:T(1024)S(1)} %copy-done.49, f32[768]{0:T(1024)S(1)} %get-tuple-element.91, ...), kind=kOutput, calls=%fused_computation.23 | convolution fusion | flops 4854644736 | bytes 26765312 | tf_op jit(solution)/shard_map/dot_general | solution.py:29
  170.8 4.8 lay.5
  175.5 9.2 %fusion.125 = (f32[1024]{0:T(1024)S(1)}, f32[1024,768]{1,0:T(8,128)S(1)}) fusion(f32[768]{0:T(1024)S(1)} %copy-done.50, bf16[1024,3072]{1,0:T(8,128)(2,1)} %get-tuple-element.148, bf16[3072,768]{1,0:T(8,128)(2,1)} %bitcast.233, f32[768]{0:T(1024)S(1)} %copy-done.49, f32[768]{0:T(1024)S(1)} %get-tuple-element.91, f32[1024]{0:T(1024)S(1)} %copy-done.45, ...), kind=kOutput, calls=%fused_computation.251 | convolution fusion | flops 4837342208 | bytes 17323008 | tf_op jit(solution)/shard_map/dot_general | solution.py:29
  185.9 3.3 fusion.25
  189.2 2.6 convert_reduce_fusion.4
  191.8 5.7 %convolution_convert_fusion.1 = bf16[3072,768]{1,0:T(8,128)(2,1)S(1)} fusion(bf16[1024,3072]{1,0:T(8,128)(2,1)S(1)} %bitcast.269, f32[1024,768]{1,0:T(8,128)S(1)} %get-tuple-element.96), kind=kOutput, calls=%fused_computation.36 | convolution fusion | flops 4834983936 | bytes 14155776 | tf_op jit(solution)/shard_map/dot_general | solution.py:29
  201.8 14.0 %convert_reduce_fusion = (bf16[3072]{0:T(1024)(128)(2,1)}, bf16[1024,3072]{1,0:T(8,128)(2,1)}) fusion(f32[1024,3072]{1,0:T(8,128)} %get-tuple-element.149, f32[3072]{0:T(1024)S(1)} %copy-done.46, bf16[3072,768]{1,0:T(8,128)(2,1)S(1)} %bitcast.236, f32[1024,768]{1,0:T(8,128)S(1)} %get-tuple-element.96), kind=kOutput, calls=%fused_computation.21 | convolution fusion | flops 4879807488 | bytes 26757120 | tf_op jit(solution)/shard_map/dot_general | solution.py:29
  219.8 9.1 %multiply_reduce_fusion.1 = (bf16[768]{0:T(1024)(128)(2,1)S(1)}, f32[1024]{0:T(1024)S(1)}, f32[1024]{0:T(1024)S(1)}, bf16[768]{0:T(1024)(128)(2,1)S(1)}, f32[1024,768]{1,0:T(8,128)S(1)}) fusion(f32[1024,768]{1,0:T(8,128)S(1)} %get-tuple-element.101, f32[1024]{0:T(1024)S(1)} %copy-done.45, f32[1024]{0:T(1024)S(1)} %broadcast_multiply_fusion.4, ...), kind=kOutput, calls=%fused_computation.65 | convolution fusion | flops 4839698432 | bytes 20469760 | tf_op jit(solution)/shard_map/dot_general | solution.py:29
  228.9 8.5 %convolution_convert_fusion = bf16[768,3072]{1,0:T(8,128)(2,1)S(1)} fusion(bf16[1024,3072]{1,0:T(8,128)(2,1)} %get-tuple-element.72, f32[1024,768]{1,0:T(8,128)S(1)} %get-tuple-element.101, f32[768]{0:T(1024)S(1)} %copy-done.49, f32[768]{0:T(1024)S(1)} %get-tuple-element.91, f32[1024]{0:T(1024)S(1)} %copy-done.45, f32[1024]{0:T(1024)S(1)} %broadcast_multiply_fusion.4), kind=kOutput, calls=%fused_computation.35 | convolution fusion | flops 4838129664 | bytes 14170112 | tf_op jit(solution)/shard_map/dot_general | solution.py:29
  241.5 2.8 collective-permute-done.33
  251.7 8.7 %collective-permute-done.34 = bf16[384,768]{1,0:T(8,128)(2,1)} collective-permute-done((bf16[384,768]{1,0:T(8,128)(2,1)}, bf16[384,768]{1,0:T(8,128)(2,1)}, u32[]{:S(2)}, u32[]{:S(2)}) %collective-permute-start.34) | collective-permute-done | bytes 589856 | tf_op jit(solution)/shard_map/ppermute | solution.py:115
  260.3 2.5 fusion.72
  264.3 8.7 %collective-permute-done.35 = bf16[384,768]{1,0:T(8,128)(2,1)} collective-permute-done((bf16[384,768]{1,0:T(8,128)(2,1)}, bf16[384,768]{1,0:T(8,128)(2,1)}, u32[]{:S(2)}, u32[]{:S(2)}) %collective-permute-start.35) | collective-permute-done | bytes 589856 | tf_op jit(solution)/shard_map/ppermute | solution.py:115
  273.0 2.5 fusion.71
  277.3 3.9 convolution_convert_fusion.2
  281.2 4.4 collective-permute-done.37
  292.2 12.0 %convert_reduce_fusion.2 = (bf16[12,64]{1,0:T(8,128)(2,1)S(1)}, bf16[2,512,12,64]{1,3,2,0:T(8,128)(2,1)}) fusion(bf16[2,12,512,64]{2,0,3,1:T(2,128)(2,1)} %bitcast.251, f32[2,12,512,512]{2,3,1,0:T(8,128)} %get-tuple-element.147, f32[2,12,512]{2,1,0:T(8,128)S(1)} %get-tuple-element.146), kind=kOutput, calls=%fused_computation.62 | convolution fusion | flops 820247808 | bytes 28362240 | tf_op jit(solution)/shard_map/rhqk,rhqd->rhkd/dot_general | solution.py:698
  304.1 16.7 %multiply_reduce_fusion = (f32[2,12,512]{2,1,0:T(8,128)S(1)}, f32[2,12,512,512]{2,3,1,0:T(8,128)}) fusion(f32[2,12,512,512]{2,3,1,0:T(8,128)} %get-tuple-element.147, f32[2,12,512]{2,1,0:T(8,128)S(1)} %get-tuple-element.146, bf16[2,12,512,64]{2,0,3,1:T(2,128)(2,1)S(1)} %bitcast.246, bf16[2,12,512,64]{2,0,3,1:T(2,128)(2,1)} %bitcast.252), kind=kOutput, calls=%fused_computation.2 | convolution fusion | flops 824168448 | bytes 53575680 | tf_op jit(solution)/shard_map/rhqd,rhkd->rhqk/dot_general | solution.py:699
  320.9 21.2 %multiply_convert_fusion = bf16[2,12,512,512]{2,3,1,0:T(8,128)(2,1)} fusion(f32[2,12,512,512]{2,3,1,0:T(8,128)} %get-tuple-element.154, f32[2,12,512]{2,1,0:T(8,128)S(1)} %get-tuple-element.153, f32[2,12,512,512]{2,3,1,0:T(8,128)} %get-tuple-element.147, f32[2,12,512]{2,1,0:T(8,128)S(1)} %get-tuple-element.146), kind=kLoop, calls=%fused_computation.1 | loop fusion | flops 25165824 | bytes 63012864 | tf_op jit(solution)/shard_map/convert_element_type | solution.py:700
  342.1 10.2 %fusion.47 = bf16[2,512,12,64]{1,3,2,0:T(8,128)(2,1)} fusion(bf16[2,12,512,512]{2,3,1,0:T(8,128)(2,1)} %multiply_convert_fusion, bf16[2,12,512,64]{2,0,3,1:T(2,128)(2,1)} %bitcast.244), kind=kOutput, calls=%fused_computation.117 | convolution fusion | flops 806879232 | bytes 15728640 | tf_op jit(solution)/shard_map/rhqk,rhqd->rhkd/dot_general | solution.py:702
  352.2 8.1 %fusion.46 = bf16[2,512,12,64]{1,3,2,0:T(8,128)(2,1)} fusion(bf16[2,12,512,512]{2,3,1,0:T(8,128)(2,1)} %multiply_convert_fusion, bf16[2,12,512,64]{2,0,3,1:T(2,128)(2,1)S(1)} %bitcast.211), kind=kOutput, calls=%fused_computation.116 | convolution fusion | flops 806879232 | bytes 15728640 | tf_op jit(solution)/shard_map/rhqk,rhkd->rhqd/dot_general | solution.py:701
  367.7 2.5 convolution_convert_fusion.4
  375.3 2.5 convolution_convert_fusion.5
  378.1 2.5 convolution_convert_fusion.6
  391.5 3.1 collective-permute-done.40
  402.1 5.7 %collective-permute-done.42 = bf16[96,3840]{1,0:T(8,128)(2,1)S(1)} collective-permute-done((bf16[96,3840]{1,0:T(8,128)(2,1)S(1)}, bf16[96,3840]{1,0:T(8,128)(2,1)S(1)}, u32[]{:S(2)}, u32[]{:S(2)}) %collective-permute-start.42) | collective-permute-done | bytes 737312 | tf_op jit(solution)/shard_map/ppermute | solution.py:115
  415.3 10.9 %collective-permute-done.47 = bf16[320,768]{1,0:T(8,128)(2,1)S(1)} collective-permute-done((bf16[320,768]{1,0:T(8,128)(2,1)S(1)}, bf16[320,768]{1,0:T(8,128)(2,1)S(1)}, u32[]{:S(2)}, u32[]{:S(2)}) %collective-permute-start.47) | collective-permute-done | bytes 491552 | tf_op jit(solution)/shard_map/ppermute | solution.py:115
  432.2 4.2 collective-permute-done.48
  441.0 5.7 %collective-permute-done.49 = bf16[320,768]{1,0:T(8,128)(2,1)S(1)} collective-permute-done((bf16[320,768]{1,0:T(8,128)(2,1)S(1)}, bf16[320,768]{1,0:T(8,128)(2,1)S(1)}, u32[]{:S(2)}, u32[]{:S(2)}) %collective-permute-start.49) | collective-permute-done | bytes 491552 | tf_op jit(solution)/shard_map/ppermute | solution.py:115
  447.9 2.8 maximum_select_fusion.1
  454.4 12.9 %collective-permute-done.54 = bf16[96,3840]{1,0:T(8,128)(2,1)S(1)} collective-permute-done((bf16[96,3840]{1,0:T(8,128)(2,1)S(1)}, bf16[96,3840]{1,0:T(8,128)(2,1)S(1)}, u32[]{:S(2)}, u32[]{:S(2)}) %collective-permute-start.54) | collective-permute-done | bytes 737312 | tf_op jit(solution)/shard_map/ppermute | solution.py:112
  469.3 8.1 %collective-permute-done.51 = bf16[320,768]{1,0:T(8,128)(2,1)S(1)} collective-permute-done((bf16[320,768]{1,0:T(8,128)(2,1)S(1)}, bf16[320,768]{1,0:T(8,128)(2,1)S(1)}, u32[]{:S(2)}, u32[]{:S(2)}) %collective-permute-start.51) | collective-permute-done | bytes 491552 | tf_op jit(solution)/shard_map/ppermute | solution.py:112
  (348 shorter events, 150.9 us)
Async XLA Ops:
  2.8 11.6 %collective-permute-start.4 = (bf16[416,768]{1,0:T(8,128)(2,1)}, bf16[416,768]{1,0:T(8,128)(2,1)}, u32[]{:S(2)}, u32[]{:S(2)}) collective-permute-start(bf16[416,768]{1,0:T(8,128)(2,1)} %pack.1.refs_1_), channel_id=1, source_target_pairs={{0,8},{1,5},{2,10},{3,7},{4,0},{5,13},{6,2},{7,15},{8,16},{9,1},{1... | collective-permute-start | bytes 1916936 | tf_op jit(solution)/shard_map/ppermute | solution.py:115
  11.7 18.2 %collective-permute-start.1 = (bf16[4,128,768]{2,1,0:T(8,128)(2,1)S(1)}, bf16[4,128,768]{2,1,0:T(8,128)(2,1)S(1)}, u32[]{:S(2)}, u32[]{:S(2)}) collective-permute-start(bf16[4,128,768]{2,1,0:T(8,128)(2,1)S(1)} %get-tuple-element.130), channel_id=1, source_target_pairs={{0,2},{1,3},{2,0},{3,1},{4,6},{5,7},{6,4},{7,5},{8,10},{9,11},{10,... | collective-permute-start | bytes 2359304 | tf_op jit(solution)/shard_map/ppermute | solution.py:112
  14.5 17.6 %collective-permute-start.5 = (bf16[416,768]{1,0:T(8,128)(2,1)}, bf16[416,768]{1,0:T(8,128)(2,1)}, u32[]{:S(2)}, u32[]{:S(2)}) collective-permute-start(bf16[416,768]{1,0:T(8,128)(2,1)} %collective-permute-done.4.refs_2_), channel_id=1, source_target_pairs={{0,8},{1,5},{2,10},{3,7},{4,0},{5,13},{6,2},{7,15},{8,16},{9,1},{1... | collective-permute-start | bytes 1916936 | tf_op jit(solution)/shard_map/ppermute | solution.py:115
  32.0 12.6 %collective-permute-start.2 = (bf16[2,256,768]{2,1,0:T(8,128)(2,1)S(1)}, bf16[2,256,768]{2,1,0:T(8,128)(2,1)S(1)}, u32[]{:S(2)}, u32[]{:S(2)}) collective-permute-start(bf16[2,256,768]{2,1,0:T(8,128)(2,1)S(1)} %get-tuple-element.128), channel_id=1, source_target_pairs={{0,1},{1,0},{2,3},{3,2},{4,5},{5,4},{6,7},{7,6},{8,9},{9,8},{10,11... | collective-permute-start | bytes 2359304 | tf_op jit(solution)/shard_map/ppermute | solution.py:112
  32.1 10.7 %collective-permute-start.6 = (bf16[416,768]{1,0:T(8,128)(2,1)}, bf16[416,768]{1,0:T(8,128)(2,1)S(1)}, u32[]{:S(2)}, u32[]{:S(2)}) collective-permute-start(bf16[416,768]{1,0:T(8,128)(2,1)} %collective-permute-done.5.refs_3_), channel_id=1, source_target_pairs={{0,8},{1,5},{2,10},{3,7},{4,0},{5,13},{6,2},{7,15},{8,16},{9,1},{1... | collective-permute-start | bytes 1916936 | tf_op jit(solution)/shard_map/ppermute | solution.py:115
  32.2 10.6 %collective-permute-start.3 = (s32[2,256]{1,0:T(2,128)S(1)}, s32[2,256]{1,0:T(2,128)S(1)}, u32[]{:S(2)}, u32[]{:S(2)}) collective-permute-start(s32[2,256]{1,0:T(2,128)S(1)} %get-tuple-element.143), channel_id=1, source_target_pairs={{0,1},{1,0},{2,3},{3,2},{4,5},{5,4},{6,7},{7,6},{8,9},{9,8},{10,11... | collective-permute-start | bytes 6152 | tf_op jit(solution)/shard_map/ppermute | solution.py:112
  34.0 22.4 %collective-permute-start.7 = (bf16[416,768]{1,0:T(8,128)(2,1)}, bf16[416,768]{1,0:T(8,128)(2,1)}, u32[]{:S(2)}, u32[]{:S(2)}) collective-permute-start(bf16[416,768]{1,0:T(8,128)(2,1)} %collective-permute-done.4.refs_2_), channel_id=1, source_target_pairs={{0,1},{1,0},{2,3},{3,2},{4,5},{5,4},{6,7},{7,6},{8,9},{9,8},{10,11... | collective-permute-start | bytes 1916936 | tf_op jit(solution)/shard_map/ppermute | solution.py:112
  34.1 24.0 %collective-permute-start.8 = (bf16[416,768]{1,0:T(8,128)(2,1)}, bf16[416,768]{1,0:T(8,128)(2,1)}, u32[]{:S(2)}, u32[]{:S(2)}) collective-permute-start(bf16[416,768]{1,0:T(8,128)(2,1)} %collective-permute-done.5.refs_3_), channel_id=1, source_target_pairs={{0,1},{1,0},{2,3},{3,2},{4,5},{5,4},{6,7},{7,6},{8,9},{9,8},{10,11... | collective-permute-start | bytes 1916936 | tf_op jit(solution)/shard_map/ppermute | solution.py:112
  42.9 13.4 %collective-permute-start.12 = (bf16[96,3072]{1,0:T(8,128)(2,1)}, bf16[96,3072]{1,0:T(8,128)(2,1)}, u32[]{:S(2)}, u32[]{:S(2)}) collective-permute-start(bf16[96,3072]{1,0:T(8,128)(2,1)} %refs_1_.4), channel_id=1, source_target_pairs={{0,8},{1,5},{2,10},{3,7},{4,0},{5,13},{6,2},{7,15},{8,16},{9,1},{1... | collective-permute-start | bytes 1769480 | tf_op jit(solution)/shard_map/ppermute | solution.py:115
  44.6 13.5 %collective-permute-start.9 = (bf16[416,768]{1,0:T(8,128)(2,1)S(1)}, bf16[416,768]{1,0:T(8,128)(2,1)}, u32[]{:S(2)}, u32[]{:S(2)}) collective-permute-start(bf16[416,768]{1,0:T(8,128)(2,1)S(1)} %collective-permute-done.6.refs_4_), channel_id=1, source_target_pairs={{0,1},{1,0},{2,3},{3,2},{4,5},{5,4},{6,7},{7,6},{8,9},{9,8},{10,11... | collective-permute-start | bytes 1916936 | tf_op jit(solution)/shard_map/ppermute | solution.py:112
  56.3 58.1 %collective-permute-start.20 = (bf16[384,768]{1,0:T(8,128)(2,1)}, bf16[384,768]{1,0:T(8,128)(2,1)}, u32[]{:S(2)}, u32[]{:S(2)}) collective-permute-start(bf16[384,768]{1,0:T(8,128)(2,1)} %refs_1_.5), channel_id=1, source_target_pairs={{0,8},{1,5},{2,10},{3,7},{4,0},{5,13},{6,2},{7,15},{8,16},{9,1},{1... | collective-permute-start | bytes 1769480 | tf_op jit(solution)/shard_map/ppermute | solution.py:115
  56.3 93.7 %collective-permute-start.15 = (bf16[96,3072]{1,0:T(8,128)(2,1)}, bf16[96,3072]{1,0:T(8,128)(2,1)}, u32[]{:S(2)}, u32[]{:S(2)}) collective-permute-start(bf16[96,3072]{1,0:T(8,128)(2,1)} %collective-permute-done.12.refs_2_), channel_id=1, source_target_pairs={{0,1},{1,0},{2,3},{3,2},{4,5},{5,4},{6,7},{7,6},{8,9},{9,8},{10,11... | collective-permute-start | bytes 1769480 | tf_op jit(solution)/shard_map/ppermute | solution.py:112
  56.4 59.7 %collective-permute-start.13 = (bf16[96,3072]{1,0:T(8,128)(2,1)}, bf16[96,3072]{1,0:T(8,128)(2,1)}, u32[]{:S(2)}, u32[]{:S(2)}) collective-permute-start(bf16[96,3072]{1,0:T(8,128)(2,1)} %collective-permute-done.12.refs_2_), channel_id=1, source_target_pairs={{0,8},{1,5},{2,10},{3,7},{4,0},{5,13},{6,2},{7,15},{8,16},{9,1},{1... | collective-permute-start | bytes 1769480 | tf_op jit(solution)/shard_map/ppermute | solution.py:115
  82.8 36.6 %collective-permute-start.30 = (bf16[4,128,768]{2,1,0:T(8,128)(2,1)}, bf16[4,128,768]{2,1,0:T(8,128)(2,1)}, u32[]{:S(2)}, u32[]{:S(2)}) collective-permute-start(bf16[4,128,768]{2,1,0:T(8,128)(2,1)} %get-tuple-element.121), channel_id=1, source_target_pairs={{0,2},{1,3},{2,0},{3,1},{4,6},{5,7},{6,4},{7,5},{8,10},{9,11},{10,... | collective-permute-start | bytes 2359304 | tf_op jit(solution)/shard_map/ppermute | solution.py:112
  114.4 19.2 %collective-permute-start.21 = (bf16[384,768]{1,0:T(8,128)(2,1)}, bf16[384,768]{1,0:T(8,128)(2,1)}, u32[]{:S(2)}, u32[]{:S(2)}) collective-permute-start(bf16[384,768]{1,0:T(8,128)(2,1)} %collective-permute-done.20.refs_2_), channel_id=1, source_target_pairs={{0,8},{1,5},{2,10},{3,7},{4,0},{5,13},{6,2},{7,15},{8,16},{9,1},{1... | collective-permute-start | bytes 1769480 | tf_op jit(solution)/shard_map/ppermute | solution.py:115
  116.1 14.9 %collective-permute-start.14 = (bf16[96,3072]{1,0:T(8,128)(2,1)}, bf16[96,3072]{1,0:T(8,128)(2,1)}, u32[]{:S(2)}, u32[]{:S(2)}) collective-permute-start(bf16[96,3072]{1,0:T(8,128)(2,1)} %collective-permute-done.13.refs_3_), channel_id=1, source_target_pairs={{0,8},{1,5},{2,10},{3,7},{4,0},{5,13},{6,2},{7,15},{8,16},{9,1},{1... | collective-permute-start | bytes 1769480 | tf_op jit(solution)/shard_map/ppermute | solution.py:115
  121.8 24.4 %collective-permute-start.31 = (bf16[2,256,768]{2,1,0:T(8,128)(2,1)}, bf16[2,256,768]{2,1,0:T(8,128)(2,1)}, u32[]{:S(2)}, u32[]{:S(2)}) collective-permute-start(bf16[2,256,768]{2,1,0:T(8,128)(2,1)} %get-tuple-element.120), channel_id=1, source_target_pairs={{0,1},{1,0},{2,3},{3,2},{4,5},{5,4},{6,7},{7,6},{8,9},{9,8},{10,11... | collective-permute-start | bytes 2359304 | tf_op jit(solution)/shard_map/ppermute | solution.py:112
  133.6 11.6 %collective-permute-start.22 = (bf16[384,768]{1,0:T(8,128)(2,1)}, bf16[384,768]{1,0:T(8,128)(2,1)}, u32[]{:S(2)}, u32[]{:S(2)}) collective-permute-start(bf16[384,768]{1,0:T(8,128)(2,1)} %collective-permute-done.21.refs_3_), channel_id=1, source_target_pairs={{0,8},{1,5},{2,10},{3,7},{4,0},{5,13},{6,2},{7,15},{8,16},{9,1},{1... | collective-permute-start | bytes 1769480 | tf_op jit(solution)/shard_map/ppermute | solution.py:115
  135.7 14.4 %collective-permute-start.16 = (bf16[96,3072]{1,0:T(8,128)(2,1)}, bf16[96,3072]{1,0:T(8,128)(2,1)}, u32[]{:S(2)}, u32[]{:S(2)}) collective-permute-start(bf16[96,3072]{1,0:T(8,128)(2,1)} %collective-permute-done.13.refs_3_), channel_id=1, source_target_pairs={{0,1},{1,0},{2,3},{3,2},{4,5},{5,4},{6,7},{7,6},{8,9},{9,8},{10,11... | collective-permute-start | bytes 1769480 | tf_op jit(solution)/shard_map/ppermute | solution.py:112
  138.8 11.8 %collective-permute-start.17 = (bf16[96,3072]{1,0:T(8,128)(2,1)}, bf16[96,3072]{1,0:T(8,128)(2,1)}, u32[]{:S(2)}, u32[]{:S(2)}) collective-permute-start(bf16[96,3072]{1,0:T(8,128)(2,1)} %collective-permute-done.14.refs_4_), channel_id=1, source_target_pairs={{0,1},{1,0},{2,3},{3,2},{4,5},{5,4},{6,7},{7,6},{8,9},{9,8},{10,11... | collective-permute-start | bytes 1769480 | tf_op jit(solution)/shard_map/ppermute | solution.py:112
  146.2 9.9 %collective-permute-start.26 = (bf16[192,768]{1,0:T(8,128)(2,1)S(1)}, bf16[192,768]{1,0:T(8,128)(2,1)S(1)}, u32[]{:S(2)}, u32[]{:S(2)}) collective-permute-start(bf16[192,768]{1,0:T(8,128)(2,1)S(1)} %constant_dynamic-slice_fusion.12), channel_id=1, source_target_pairs={{0,8},{1,5},{2,10},{3,7},{4,0},{5,13},{6,2},{7,15},{8,16},{9,1},{1... | collective-permute-start | bytes 884744 | tf_op jit(solution)/shard_map/ppermute | solution.py:115
  150.0 18.9 %collective-permute-start.23 = (bf16[384,768]{1,0:T(8,128)(2,1)}, bf16[384,768]{1,0:T(8,128)(2,1)S(1)}, u32[]{:S(2)}, u32[]{:S(2)}) collective-permute-start(bf16[384,768]{1,0:T(8,128)(2,1)} %collective-permute-done.20.refs_2_), channel_id=1, source_target_pairs={{0,1},{1,0},{2,3},{3,2},{4,5},{5,4},{6,7},{7,6},{8,9},{9,8},{10,11... | collective-permute-start | bytes 1769480 | tf_op jit(solution)/shard_map/ppermute | solution.py:112
  150.1 18.8 %collective-permute-start.24 = (bf16[384,768]{1,0:T(8,128)(2,1)}, bf16[384,768]{1,0:T(8,128)(2,1)S(1)}, u32[]{:S(2)}, u32[]{:S(2)}) collective-permute-start(bf16[384,768]{1,0:T(8,128)(2,1)} %collective-permute-done.21.refs_3_), channel_id=1, source_target_pairs={{0,1},{1,0},{2,3},{3,2},{4,5},{5,4},{6,7},{7,6},{8,9},{9,8},{10,11... | collective-permute-start | bytes 1769480 | tf_op jit(solution)/shard_map/ppermute | solution.py:112
  150.6 18.3 %collective-permute-start.25 = (bf16[384,768]{1,0:T(8,128)(2,1)}, bf16[384,768]{1,0:T(8,128)(2,1)S(1)}, u32[]{:S(2)}, u32[]{:S(2)}) collective-permute-start(bf16[384,768]{1,0:T(8,128)(2,1)} %collective-permute-done.22.refs_4_), channel_id=1, source_target_pairs={{0,1},{1,0},{2,3},{3,2},{4,5},{5,4},{6,7},{7,6},{8,9},{9,8},{10,11... | collective-permute-start | bytes 1769480 | tf_op jit(solution)/shard_map/ppermute | solution.py:112
  156.1 12.8 %collective-permute-start.27 = (bf16[192,768]{1,0:T(8,128)(2,1)S(1)}, bf16[192,768]{1,0:T(8,128)(2,1)S(1)}, u32[]{:S(2)}, u32[]{:S(2)}) collective-permute-start(bf16[192,768]{1,0:T(8,128)(2,1)S(1)} %collective-permute-done.26.refs_8_), channel_id=1, source_target_pairs={{0,1},{1,0},{2,3},{3,2},{4,5},{5,4},{6,7},{7,6},{8,9},{9,8},{10,11... | collective-permute-start | bytes 884744 | tf_op jit(solution)/shard_map/ppermute | solution.py:112
  198.5 17.3 %collective-permute-start.28 = (bf16[2,256,768]{2,1,0:T(8,128)(2,1)}, bf16[2,256,768]{2,1,0:T(8,128)(2,1)}, u32[]{:S(2)}, u32[]{:S(2)}) collective-permute-start(bf16[2,256,768]{2,1,0:T(8,128)(2,1)} %get-tuple-element.126), channel_id=1, source_target_pairs={{0,1},{1,0},{2,3},{3,2},{4,5},{5,4},{6,7},{7,6},{8,9},{9,8},{10,11... | collective-permute-start | bytes 2359304 | tf_op jit(solution)/shard_map/ppermute | solution.py:112
  199.1 20.7 %collective-permute-start.32 = (bf16[4,384,768]{2,1,0:T(8,128)(2,1)S(1)}, bf16[4,384,768]{2,1,0:T(8,128)(2,1)S(1)}, u32[]{:S(2)}, u32[]{:S(2)}) collective-permute-start(bf16[4,384,768]{2,1,0:T(8,128)(2,1)S(1)} %pad_maximum_fusion.1), channel_id=1, source_target_pairs={{0,1},{1,0},{2,3},{3,2},{4,5},{5,4},{6,7},{7,6},{8,9},{9,8},{10,11... | collective-permute-start | bytes 7077896 | tf_op jit(solution)/shard_map/ppermute | solution.py:112
  218.7 22.8 %collective-permute-start.29 = (bf16[4,128,768]{2,1,0:T(8,128)(2,1)}, bf16[4,128,768]{2,1,0:T(8,128)(2,1)}, u32[]{:S(2)}, u32[]{:S(2)}) collective-permute-start(bf16[4,128,768]{2,1,0:T(8,128)(2,1)} %get-tuple-element.124), channel_id=1, source_target_pairs={{0,2},{1,3},{2,0},{3,1},{4,6},{5,7},{6,4},{7,5},{8,10},{9,11},{10,... | collective-permute-start | bytes 2359304 | tf_op jit(solution)/shard_map/ppermute | solution.py:112
  247.8 40.0 %collective-permute-start.36 = (bf16[4,96,3840]{2,1,0:T(8,128)(2,1)}, bf16[4,96,3840]{2,1,0:T(8,128)(2,1)}, u32[]{:S(2)}, u32[]{:S(2)}) collective-permute-start(bf16[4,96,3840]{2,1,0:T(8,128)(2,1)} %pad_maximum_fusion), channel_id=1, source_target_pairs={{0,1},{1,0},{2,3},{3,2},{4,5},{5,4},{6,7},{7,6},{8,9},{9,8},{10,11... | collective-permute-start | bytes 8847368 | tf_op jit(solution)/shard_map/ppermute | solution.py:112
  250.1 10.2 %collective-permute-start.34 = (bf16[384,768]{1,0:T(8,128)(2,1)}, bf16[384,768]{1,0:T(8,128)(2,1)}, u32[]{:S(2)}, u32[]{:S(2)}) collective-permute-start(bf16[384,768]{1,0:T(8,128)(2,1)} %fusion.73), channel_id=1, source_target_pairs={{0,8},{1,5},{2,10},{3,7},{4,0},{5,13},{6,2},{7,15},{8,16},{9,1},{1... | collective-permute-start | bytes 1769480 | tf_op jit(solution)/shard_map/ppermute | solution.py:115
  262.8 10.2 %collective-permute-start.35 = (bf16[384,768]{1,0:T(8,128)(2,1)}, bf16[384,768]{1,0:T(8,128)(2,1)}, u32[]{:S(2)}, u32[]{:S(2)}) collective-permute-start(bf16[384,768]{1,0:T(8,128)(2,1)} %fusion.72), channel_id=1, source_target_pairs={{0,8},{1,5},{2,10},{3,7},{4,0},{5,13},{6,2},{7,15},{8,16},{9,1},{1... | collective-permute-start | bytes 1769480 | tf_op jit(solution)/shard_map/ppermute | solution.py:115
  275.4 10.2 %collective-permute-start.37 = (bf16[384,768]{1,0:T(8,128)(2,1)}, bf16[384,768]{1,0:T(8,128)(2,1)}, u32[]{:S(2)}, u32[]{:S(2)}) collective-permute-start(bf16[384,768]{1,0:T(8,128)(2,1)} %fusion.71), channel_id=1, source_target_pairs={{0,8},{1,5},{2,10},{3,7},{4,0},{5,13},{6,2},{7,15},{8,16},{9,1},{1... | collective-permute-start | bytes 1769480 | tf_op jit(solution)/shard_map/ppermute | solution.py:115
  287.8 100.2 %collective-permute-start.39 = (bf16[384,768]{1,0:T(8,128)(2,1)}, bf16[384,768]{1,0:T(8,128)(2,1)}, u32[]{:S(2)}, u32[]{:S(2)}) collective-permute-start(bf16[384,768]{1,0:T(8,128)(2,1)} %fusion.70), channel_id=1, source_target_pairs={{0,1},{1,0},{2,3},{3,2},{4,5},{5,4},{6,7},{7,6},{8,9},{9,8},{10,11... | collective-permute-start | bytes 1769480 | tf_op jit(solution)/shard_map/ppermute | solution.py:112
  362.4 15.4 %collective-permute-start.38 = (bf16[48,3840]{1,0:T(8,128)(2,1)}, bf16[48,3840]{1,0:T(8,128)(2,1)S(1)}, u32[]{:S(2)}, u32[]{:S(2)}) collective-permute-start(bf16[48,3840]{1,0:T(8,128)(2,1)} %fusion.91), channel_id=1, source_target_pairs={{0,8},{1,5},{2,10},{3,7},{4,0},{5,13},{6,2},{7,15},{8,16},{9,1},{1... | collective-permute-start | bytes 1105928 | tf_op jit(solution)/shard_map/ppermute | solution.py:115
  382.9 11.8 %collective-permute-start.40 = (bf16[96,3840]{1,0:T(8,128)(2,1)}, bf16[96,3840]{1,0:T(8,128)(2,1)}, u32[]{:S(2)}, u32[]{:S(2)}) collective-permute-start(bf16[96,3840]{1,0:T(8,128)(2,1)} %fusion.51), channel_id=1, source_target_pairs={{0,8},{1,5},{2,10},{3,7},{4,0},{5,13},{6,2},{7,15},{8,16},{9,1},{1... | collective-permute-start | bytes 2211848 | tf_op jit(solution)/shard_map/ppermute | solution.py:115
  387.9 13.3 %collective-permute-start.43 = (bf16[4,320,768]{2,1,0:T(8,128)(2,1)S(1)}, bf16[4,320,768]{2,1,0:T(8,128)(2,1)S(1)}, u32[]{:S(2)}, u32[]{:S(2)}) collective-permute-start(bf16[4,320,768]{2,1,0:T(8,128)(2,1)S(1)} %pad_maximum_fusion.2), channel_id=1, source_target_pairs={{0,1},{1,0},{2,3},{3,2},{4,5},{5,4},{6,7},{7,6},{8,9},{9,8},{10,11... | collective-permute-start | bytes 5898248 | tf_op jit(solution)/shard_map/ppermute | solution.py:112
  390.4 23.8 %collective-permute-start.41 = (bf16[384,768]{1,0:T(8,128)(2,1)S(1)}, bf16[384,768]{1,0:T(8,128)(2,1)S(1)}, u32[]{:S(2)}, u32[]{:S(2)}) collective-permute-start(bf16[384,768]{1,0:T(8,128)(2,1)S(1)} %add_convert_fusion.5), channel_id=1, source_target_pairs={{0,2},{1,3},{2,0},{3,1},{4,6},{5,7},{6,4},{7,5},{8,10},{9,11},{10,... | collective-permute-start | bytes 1769480 | tf_op jit(solution)/shard_map/ppermute | solution.py:112
  396.3 11.5 %collective-permute-start.42 = (bf16[96,3840]{1,0:T(8,128)(2,1)S(1)}, bf16[96,3840]{1,0:T(8,128)(2,1)S(1)}, u32[]{:S(2)}, u32[]{:S(2)}) collective-permute-start(bf16[96,3840]{1,0:T(8,128)(2,1)S(1)} %fusion.50), channel_id=1, source_target_pairs={{0,8},{1,5},{2,10},{3,7},{4,0},{5,13},{6,2},{7,15},{8,16},{9,1},{1... | collective-permute-start | bytes 2211848 | tf_op jit(solution)/shard_map/ppermute | solution.py:115
  401.4 10.0 %collective-permute-start.46 = (bf16[160,768]{1,0:T(8,128)(2,1)S(1)}, bf16[160,768]{1,0:T(8,128)(2,1)S(1)}, u32[]{:S(2)}, u32[]{:S(2)}) collective-permute-start(bf16[160,768]{1,0:T(8,128)(2,1)S(1)} %fusion.93), channel_id=1, source_target_pairs={{0,8},{1,5},{2,10},{3,7},{4,0},{5,13},{6,2},{7,15},{8,16},{9,1},{1... | collective-permute-start | bytes 737288 | tf_op jit(solution)/shard_map/ppermute | solution.py:115
  409.4 19.6 %collective-permute-start.52 = (bf16[96,3840]{1,0:T(8,128)(2,1)S(1)}, bf16[96,3840]{1,0:T(8,128)(2,1)S(1)}, u32[]{:S(2)}, u32[]{:S(2)}) collective-permute-start(bf16[96,3840]{1,0:T(8,128)(2,1)S(1)} %fusion.49), channel_id=1, source_target_pairs={{0,8},{1,5},{2,10},{3,7},{4,0},{5,13},{6,2},{7,15},{8,16},{9,1},{1... | collective-permute-start | bytes 2211848 | tf_op jit(solution)/shard_map/ppermute | solution.py:115
  411.6 14.6 %collective-permute-start.47 = (bf16[320,768]{1,0:T(8,128)(2,1)S(1)}, bf16[320,768]{1,0:T(8,128)(2,1)S(1)}, u32[]{:S(2)}, u32[]{:S(2)}) collective-permute-start(bf16[320,768]{1,0:T(8,128)(2,1)S(1)} %fusion.75), channel_id=1, source_target_pairs={{0,8},{1,5},{2,10},{3,7},{4,0},{5,13},{6,2},{7,15},{8,16},{9,1},{1... | collective-permute-start | bytes 1474568 | tf_op jit(solution)/shard_map/ppermute | solution.py:115
  415.3 14.1 %collective-permute-start.44 = (bf16[2,256,768]{2,1,0:T(8,128)(2,1)}, bf16[2,256,768]{2,1,0:T(8,128)(2,1)}, u32[]{:S(2)}, u32[]{:S(2)}) collective-permute-start(bf16[2,256,768]{2,1,0:T(8,128)(2,1)} %get-tuple-element.118), channel_id=1, source_target_pairs={{0,1},{1,0},{2,3},{3,2},{4,5},{5,4},{6,7},{7,6},{8,9},{9,8},{10,11... | collective-permute-start | bytes 2359304 | tf_op jit(solution)/shard_map/ppermute | solution.py:112
  427.2 9.1 %collective-permute-start.48 = (bf16[320,768]{1,0:T(8,128)(2,1)}, bf16[320,768]{1,0:T(8,128)(2,1)}, u32[]{:S(2)}, u32[]{:S(2)}) collective-permute-start(bf16[320,768]{1,0:T(8,128)(2,1)} %fusion.76), channel_id=1, source_target_pairs={{0,8},{1,5},{2,10},{3,7},{4,0},{5,13},{6,2},{7,15},{8,16},{9,1},{1... | collective-permute-start | bytes 1474568 | tf_op jit(solution)/shard_map/ppermute | solution.py:115
  429.2 10.5 %collective-permute-start.53 = (bf16[96,3840]{1,0:T(8,128)(2,1)S(1)}, bf16[96,3840]{1,0:T(8,128)(2,1)S(1)}, u32[]{:S(2)}, u32[]{:S(2)}) collective-permute-start(bf16[96,3840]{1,0:T(8,128)(2,1)S(1)} %fusion.48), channel_id=1, source_target_pairs={{0,1},{1,0},{2,3},{3,2},{4,5},{5,4},{6,7},{7,6},{8,9},{9,8},{10,11... | collective-permute-start | bytes 2211848 | tf_op jit(solution)/shard_map/ppermute | solution.py:112
  431.1 20.8 %collective-permute-start.45 = (bf16[4,128,768]{2,1,0:T(8,128)(2,1)S(1)}, bf16[4,128,768]{2,1,0:T(8,128)(2,1)S(1)}, u32[]{:S(2)}, u32[]{:S(2)}) collective-permute-start(bf16[4,128,768]{2,1,0:T(8,128)(2,1)S(1)} %get-tuple-element.116), channel_id=1, source_target_pairs={{0,2},{1,3},{2,0},{3,1},{4,6},{5,7},{6,4},{7,5},{8,10},{9,11},{10,... | collective-permute-start | bytes 2359304 | tf_op jit(solution)/shard_map/ppermute | solution.py:112
  437.8 8.9 %collective-permute-start.49 = (bf16[320,768]{1,0:T(8,128)(2,1)S(1)}, bf16[320,768]{1,0:T(8,128)(2,1)S(1)}, u32[]{:S(2)}, u32[]{:S(2)}) collective-permute-start(bf16[320,768]{1,0:T(8,128)(2,1)S(1)} %fusion.77), channel_id=1, source_target_pairs={{0,8},{1,5},{2,10},{3,7},{4,0},{5,13},{6,2},{7,15},{8,16},{9,1},{1... | collective-permute-start | bytes 1474568 | tf_op jit(solution)/shard_map/ppermute | solution.py:115
  440.0 27.3 %collective-permute-start.54 = (bf16[96,3840]{1,0:T(8,128)(2,1)S(1)}, bf16[96,3840]{1,0:T(8,128)(2,1)S(1)}, u32[]{:S(2)}, u32[]{:S(2)}) collective-permute-start(bf16[96,3840]{1,0:T(8,128)(2,1)S(1)} %add_convert_fusion.4), channel_id=1, source_target_pairs={{0,2},{1,3},{2,0},{3,1},{4,6},{5,7},{6,4},{7,5},{8,10},{9,11},{10,... | collective-permute-start | bytes 2211848 | tf_op jit(solution)/shard_map/ppermute | solution.py:112
  453.4 24.1 %collective-permute-start.51 = (bf16[320,768]{1,0:T(8,128)(2,1)S(1)}, bf16[320,768]{1,0:T(8,128)(2,1)S(1)}, u32[]{:S(2)}, u32[]{:S(2)}) collective-permute-start(bf16[320,768]{1,0:T(8,128)(2,1)S(1)} %add_convert_fusion.6), channel_id=1, source_target_pairs={{0,2},{1,3},{2,0},{3,1},{4,6},{5,7},{6,4},{7,5},{8,10},{9,11},{10,... | collective-permute-start | bytes 1474568 | tf_op jit(solution)/shard_map/ppermute | solution.py:112
  (74 other events, 637.2 us)
